TPU v7x, 512 devices: a whole 4x4x16 slice. The times are simulated.
512 devices in a mesh: dp: 2 (over y_lo), tm: 256 (over y_hi, x, z, core).
Axes of the slice: x: 4, y: 4 (y_hi: 2, y_lo: 2; y = y_hi * 2 + y_lo), z: 16, core: 2. Of those that a mesh axis runs over, the one named last changes fastest.
Arguments:
- inputs: bfloat16 [2, 262144, 256], P('dp', 'tm'), may hold values from -6 to 6
- cotangent: bfloat16 [2, 262144, 256], P('dp', 'tm'), may hold values from -6 to 6
- first_filter_weight: bfloat16 [2, 256, 512], replicated, may hold values from -0.25 to 0.25
- first_residual_matrix: bfloat16 [256, 256], replicated, may hold values from -0.375 to 0.375
- second_filter_weight: bfloat16 [2, 256, 512], replicated, may hold values from -0.25 to 0.25
- second_residual_matrix: bfloat16 [256, 256], replicated, may hold values from -0.375 to 0.375
Outputs:
- gradient_by_input: bfloat16 [2, 262144, 256], P('dp', 'tm')
- grads_first: float32 [327680], P(('dp', 'tm'))
- grads_second: float32 [327680], P(('dp', 'tm'))
All inputs are finite; a program needn't handle non-finite values.
Results may differ from a plain program's by a relative error of at most 0.008.
Values may be sent and summed in bfloat16 or wider, within the bound.
No kernel may reach another device: no remote copies, remote signals or barrier semaphores. Data moves between devices by JAX's collectives and lax.ppermute only.
A program may use at most 64 MiB of HBM per device.

v0:
```python
import jax
import jax.numpy as jnp
from jax import lax
from jax.sharding import PartitionSpec as P


def from_behind(block, axis, distance):
    devices = range(lax.axis_size(axis))
    route = [(i - distance, i) for i in devices if i - distance in devices]
    return lax.ppermute(block, axis, route)


def contract_rows(left, right):
    return lax.dot_general(
        left, right, (((0,), (0,)), ((), ())), preferred_element_type=jnp.float32
    )


def contract_cols(left, right):
    return lax.dot_general(
        left, right, (((1,), (1,)), ((), ())), preferred_element_type=jnp.float32
    )


def gate_forward(current, earlier, conv_weight):
    pre = jnp.dot(earlier, conv_weight[0], preferred_element_type=jnp.float32) + jnp.dot(
        current, conv_weight[1], preferred_element_type=jnp.float32
    )
    half_width = pre.shape[1] // 2
    gated = (jnp.tanh(pre[:, :half_width]) * jax.nn.sigmoid(pre[:, half_width:])).astype(
        jnp.bfloat16
    )
    return (pre, gated)


def gate_backward(current, earlier, conv_weight, out_weight, pre, gated, grad_out):
    half_width = pre.shape[1] // 2
    tanh_part = jnp.tanh(pre[:, :half_width])
    sig_part = jax.nn.sigmoid(pre[:, half_width:])
    grad_gated = contract_cols(grad_out, out_weight)
    grad_pre = jnp.concatenate(
        [
            grad_gated * sig_part * (1.0 - tanh_part * tanh_part),
            grad_gated * tanh_part * sig_part * (1.0 - sig_part),
        ],
        axis=1,
    ).astype(jnp.bfloat16)
    grad_conv = jnp.stack([contract_rows(earlier, grad_pre), contract_rows(current, grad_pre)])
    grad_proj = contract_rows(gated, grad_out)
    direct = grad_out.astype(jnp.float32) + contract_cols(grad_pre, conv_weight[1])
    return (grad_conv, grad_proj, grad_pre, direct)


def per_device(
    inputs,
    cotangent,
    first_filter_weight,
    first_residual_matrix,
    second_filter_weight,
    second_residual_matrix,
):
    streams_here, length, channels = inputs.shape
    row_count = streams_here * length
    cycle_size = lax.axis_size("tm")
    near_span = min(8, cycle_size // 16)
    far_span = min(32, cycle_size // 4)
    norm_factor = float(row_count * lax.axis_size("dp") * cycle_size) ** (-0.5)
    current_first = inputs.reshape(row_count, channels)
    earlier_first = from_behind(inputs, "tm", near_span).reshape(row_count, channels)
    pre_first, gated_first = gate_forward(current_first, earlier_first, first_filter_weight)
    between_layers = (
        current_first.astype(jnp.float32)
        + jnp.dot(gated_first, first_residual_matrix, preferred_element_type=jnp.float32)
    ).astype(jnp.bfloat16)
    earlier_second = from_behind(
        between_layers.reshape(streams_here, length, channels), "tm", far_span
    ).reshape(row_count, channels)
    pre_second, gated_second = gate_forward(between_layers, earlier_second, second_filter_weight)
    grad_top = cotangent.reshape(row_count, channels)
    second_filter_gradient, second_residual_gradient, grad_pre_second, direct_second = (
        gate_backward(
            between_layers,
            earlier_second,
            second_filter_weight,
            second_residual_matrix,
            pre_second,
            gated_second,
            grad_top,
        )
    )
    arrived_second = from_behind(grad_pre_second.reshape(streams_here, length, -1), "tm", -far_span)
    back_second = contract_cols(
        arrived_second.reshape(row_count, -1), second_filter_weight[0]
    ).astype(jnp.bfloat16)
    between_layers_gradient = (direct_second + back_second.astype(jnp.float32)).astype(jnp.bfloat16)
    first_filter_gradient, first_residual_gradient, grad_pre_first, direct_first = gate_backward(
        current_first,
        earlier_first,
        first_filter_weight,
        first_residual_matrix,
        pre_first,
        gated_first,
        between_layers_gradient,
    )
    arrived_first = from_behind(grad_pre_first.reshape(streams_here, length, -1), "tm", -near_span)
    back_first = contract_cols(arrived_first.reshape(row_count, -1), first_filter_weight[0]).astype(
        jnp.bfloat16
    )
    gradient_by_input = (direct_first + back_first.astype(jnp.float32)).astype(jnp.bfloat16)
    terms_first = (
        jnp.concatenate([first_filter_gradient.reshape(-1), first_residual_gradient.reshape(-1)])
        * norm_factor
    )
    terms_second = (
        jnp.concatenate([second_filter_gradient.reshape(-1), second_residual_gradient.reshape(-1)])
        * norm_factor
    )
    grads_first, grads_second = (
        lax.psum_scatter(terms_first, ("dp", "tm"), scatter_dimension=0, tiled=True),
        lax.psum_scatter(terms_second, ("dp", "tm"), scatter_dimension=0, tiled=True),
    )
    return (gradient_by_input.reshape(inputs.shape), grads_first, grads_second)


def solution(mesh):
    in_specs = (P("dp", "tm", None), P("dp", "tm", None), P(), P(), P(), P())
    out_specs = (P("dp", "tm", None), P(("dp", "tm")), P(("dp", "tm")))
    return jax.shard_map(
        per_device, mesh=mesh, in_specs=in_specs, out_specs=out_specs, check_vma=False
    )
```

profile of v0, /device:TPU:6, one launch (start us, length us, event | category | flops | bytes accessed | tf_op | source)
XLA Modules:
  0.0 648.9 jit_solution(16213321218732052668)
XLA Ops:
  7.2 0.0 copy-start
  7.2 0.0 copy-start.5
  7.2 0.0 all-reduce.5.cloned.1.call-start
  7.2 9.2 %collective-permute-start = (bf16[1,1024,256]{2,1,0:T(8,128)(2,1)}, bf16[1,1024,256]{2,1,0:T(8,128)(2,1)S(1)}, u32[]{:S(2)}, u32[]{:S(2)}) collective-permute-start(bf16[1,1024,256]{2,1,0:T(8,128)(2,1)} %param.6), channel_id=1, source_target_pairs={{0,8},{1,9},{2,10},{3,11},{4,12},{5,13},{6,14},{7,15},{8,16},{9,17... | collective-permute-start | bytes 1572872 | tf_op jit(solution)/shard_map/ppermute | solution.py:10
  16.5 1.6 fusion.21
  18.1 23.5 %collective-permute-done = bf16[1,1024,256]{2,1,0:T(8,128)(2,1)S(1)} collective-permute-done((bf16[1,1024,256]{2,1,0:T(8,128)(2,1)}, bf16[1,1024,256]{2,1,0:T(8,128)(2,1)S(1)}, u32[]{:S(2)}, u32[]{:S(2)}) %collective-permute-start) | collective-permute-done | bytes 524320 | tf_op jit(solution)/shard_map/ppermute | solution.py:10
  41.6 0.0 copy-done.5
  41.6 0.5 convolution_add_fusion.1
  42.1 0.0 copy-start.1
  42.1 0.0 copy-start.4
  42.1 0.4 multiply_convert_fusion.5
  42.5 0.0 copy-done
  42.5 0.6 copy-done.1
  43.1 0.4 fusion.6
  43.5 6.6 %collective-permute-start.1 = (bf16[1,1024,256]{2,1,0:T(8,128)(2,1)S(1)}, bf16[1,1024,256]{2,1,0:T(8,128)(2,1)S(1)}, u32[]{:S(2)}, u32[]{:S(2)}) collective-permute-start(bf16[1,1024,256]{2,1,0:T(8,128)(2,1)S(1)} %bitcast.92), channel_id=1, source_target_pairs={{0,32},{1,33},{2,34},{3,35},{4,36},{5,37},{6,38},{7,39},{8,40},{9,... | collective-permute-start | bytes 1572872 | tf_op jit(solution)/shard_map/ppermute | solution.py:10
  50.1 0.0 copy-done.4
  50.1 0.5 fusion.27
  50.6 0.0 copy-start.12
  50.6 0.0 copy-start.13
  50.6 7.6 %collective-permute-done.1 = bf16[1,1024,256]{2,1,0:T(8,128)(2,1)S(1)} collective-permute-done((bf16[1,1024,256]{2,1,0:T(8,128)(2,1)S(1)}, bf16[1,1024,256]{2,1,0:T(8,128)(2,1)S(1)}, u32[]{:S(2)}, u32[]{:S(2)}) %collective-permute-start.1) | collective-permute-done | bytes 524320 | tf_op jit(solution)/shard_map/ppermute | solution.py:10
  58.2 0.5 convolution_add_fusion
  58.7 0.0 copy-done.12
  58.7 0.0 copy-done.13
  58.7 0.7 multiply_convert_fusion.4
  59.4 0.1 pad_maximum_fusion.1
  59.5 1.9 collective-permute-start.2
  61.4 0.5 convolution_bitcast_fusion
  61.9 0.5 convolution_bitcast_fusion.1
  62.4 0.1 pad_maximum_fusion.5
  62.5 0.3 copy.13
  62.8 0.5 convolution_bitcast_fusion.4
  63.3 0.1 copy.14
  63.5 0.5 convolution_add_fusion.4
  64.0 22.7 %collective-permute-done.2 = bf16[1,1024,512]{1,2,0:T(8,128)(2,1)S(1)} collective-permute-done((bf16[1,1024,512]{1,2,0:T(8,128)(2,1)S(1)}, bf16[1,1024,512]{1,2,0:T(8,128)(2,1)S(1)}, u32[]{:S(2)}, u32[]{:S(2)}) %collective-permute-start.2) | collective-permute-done | bytes 1048608 | tf_op jit(solution)/shard_map/ppermute | solution.py:10
  86.7 0.5 fusion.4
  87.2 0.0 copy-start.2
  87.2 0.7 multiply_convert_fusion.2
  87.9 0.1 copy-done.2
  88.0 0.0 copy-start.8
  88.0 0.3 convolution_bitcast_fusion.5
  88.3 0.8 copy.12
  89.1 0.4 convolution_bitcast_fusion.2
  89.6 0.0 copy-done.8
  89.6 0.4 convolution_bitcast_fusion.3
  90.0 0.0 copy-done.10
  90.0 0.1 pad_maximum_fusion.4
  90.1 0.3 copy.10
  90.5 0.0 copy-start.7
  90.5 0.3 copy.11
  90.8 0.7 copy-done.7
  91.4 1.8 maximum_multiply_fusion
  93.2 0.0 all-reduce.5.cloned.1.call-update
  93.2 1.0 copy-done.9
  94.2 0.2 copy-done.11
  94.4 0.1 pad_maximum_fusion.3
  94.5 29.4 %collective-permute-start.3 = (bf16[1,1024,512]{1,2,0:T(8,128)(2,1)S(1)}, bf16[1,1024,512]{1,2,0:T(8,128)(2,1)S(1)}, u32[]{:S(2)}, u32[]{:S(2)}) collective-permute-start(bf16[1,1024,512]{1,2,0:T(8,128)(2,1)S(1)} %pad_maximum_fusion.3), channel_id=1, source_target_pairs={{8,0},{9,1},{10,2},{11,3},{12,4},{13,5},{14,6},{15,7},{16,8},{17,9... | collective-permute-start | bytes 3145736 | tf_op jit(solution)/shard_map/ppermute | solution.py:10
  123.9 0.0 copy-done.3
  123.9 0.0 copy-done.6
  123.9 1.7 convolution_add_fusion.3
  125.6 86.8 %collective-permute-done.3 = bf16[1,1024,512]{1,2,0:T(8,128)(2,1)S(1)} collective-permute-done((bf16[1,1024,512]{1,2,0:T(8,128)(2,1)S(1)}, bf16[1,1024,512]{1,2,0:T(8,128)(2,1)S(1)}, u32[]{:S(2)}, u32[]{:S(2)}) %collective-permute-start.3) | collective-permute-done | bytes 1048608 | tf_op jit(solution)/shard_map/ppermute | solution.py:10
  212.3 1.3 fusion.7
  213.6 425.7 %all-reduce.5.cloned.1.call-done = (f32[327680]{0:T(1024)}, f32[327680]{0:T(1024)}) async-done(((f32[327680]{0:T(1024)}, f32[327680]{0:T(1024)}), (f32[327680]{0:T(1024)}, f32[327680]{0:T(1024)})) %all-reduce.5.cloned.1.call-update) | async-done | bytes 2621456
  639.3 1.4 dynamic-slice
  640.7 1.4 dynamic-slice.1
  (5 shorter events, 0.0 us)
Async XLA Ops:
  7.2 35.3 %copy-start = (bf16[256,256]{1,0:T(8,128)(2,1)S(1)}, bf16[256,256]{1,0:T(8,128)(2,1)}, u32[]{:S(2)}) copy-start(bf16[256,256]{1,0:T(8,128)(2,1)} %param.9) | copy-start | bytes 393220
  7.2 34.4 %copy-start.5 = (bf16[2,256,512]{2,1,0:T(8,128)(2,1)S(1)}, bf16[2,256,512]{2,1,0:T(8,128)(2,1)}, u32[]{:S(2)}) copy-start(bf16[2,256,512]{2,1,0:T(8,128)(2,1)} %param.8) | copy-start | bytes 1572868
  7.2 632.1 %all-reduce.5.cloned.1.call-start = ((), (), s32[]{:S(2)}) async-start(), calls=%async_computation | async-start | bytes 5242880
  7.2 34.3 %collective-permute-start = (bf16[1,1024,256]{2,1,0:T(8,128)(2,1)}, bf16[1,1024,256]{2,1,0:T(8,128)(2,1)S(1)}, u32[]{:S(2)}, u32[]{:S(2)}) collective-permute-start(bf16[1,1024,256]{2,1,0:T(8,128)(2,1)} %param.6), channel_id=1, source_target_pairs={{0,8},{1,9},{2,10},{3,11},{4,12},{5,13},{6,14},{7,15},{8,16},{9,17... | collective-permute-start | bytes 1572872 | tf_op jit(solution)/shard_map/ppermute | solution.py:10
  42.1 1.0 copy-start.1
  42.1 8.0 %copy-start.4 = (bf16[2,256,512]{2,1,0:T(8,128)(2,1)S(1)}, bf16[2,256,512]{2,1,0:T(8,128)(2,1)}, u32[]{:S(2)}) copy-start(bf16[2,256,512]{2,1,0:T(8,128)(2,1)} %param.10) | copy-start | bytes 1572868
  43.5 14.7 %collective-permute-start.1 = (bf16[1,1024,256]{2,1,0:T(8,128)(2,1)S(1)}, bf16[1,1024,256]{2,1,0:T(8,128)(2,1)S(1)}, u32[]{:S(2)}, u32[]{:S(2)}) collective-permute-start(bf16[1,1024,256]{2,1,0:T(8,128)(2,1)S(1)} %bitcast.92), channel_id=1, source_target_pairs={{0,32},{1,33},{2,34},{3,35},{4,36},{5,37},{6,38},{7,39},{8,40},{9,... | collective-permute-start | bytes 1572872 | tf_op jit(solution)/shard_map/ppermute | solution.py:10
  50.6 8.1 %copy-start.12 = (bf16[1,1024,256]{2,1,0:T(8,128)(2,1)S(1)}, bf16[1,1024,256]{2,1,0:T(8,128)(2,1)}, u32[]{:S(2)}) copy-start(bf16[1,1024,256]{2,1,0:T(8,128)(2,1)} %param.7) | copy-start | bytes 1572868
  50.6 8.1 %copy-start.13 = (bf16[256,256]{1,0:T(8,128)(2,1)S(1)}, bf16[256,256]{1,0:T(8,128)(2,1)}, u32[]{:S(2)}) copy-start(bf16[256,256]{1,0:T(8,128)(2,1)} %param.11) | copy-start | bytes 393220
  59.5 27.2 %collective-permute-start.2 = (bf16[1,1024,512]{1,2,0:T(8,128)(2,1)S(1)}, bf16[1,1024,512]{1,2,0:T(8,128)(2,1)S(1)}, u32[]{:S(2)}, u32[]{:S(2)}) collective-permute-start(bf16[1,1024,512]{1,2,0:T(8,128)(2,1)S(1)} %pad_maximum_fusion.1), channel_id=1, source_target_pairs={{32,0},{33,1},{34,2},{35,3},{36,4},{37,5},{38,6},{39,7},{40,8},{41... | collective-permute-start | bytes 3145736 | tf_op jit(solution)/shard_map/ppermute | solution.py:10
  87.2 0.8 copy-start.2
  88.0 1.6 copy-start.8
  88.0 2.1 copy-start.10
  90.5 1.0 copy-start.7
  93.2 1.0 copy-start.9
  93.2 1.2 copy-start.11
  93.2 30.7 %copy-start.3 = (bf16[1024,256]{1,0:T(8,128)(2,1)S(1)}, bf16[1024,256]{1,0:T(8,128)(2,1)}, u32[]{:S(2)}) copy-start(bf16[1024,256]{1,0:T(8,128)(2,1)} %copy-done.2) | copy-start | bytes 1572868
  93.2 30.7 %copy-start.6 = (bf16[2,256,512]{2,1,0:T(8,128)(2,1)S(1)}, bf16[2,256,512]{2,1,0:T(8,128)(2,1)}, u32[]{:S(2)}) copy-start(bf16[2,256,512]{2,1,0:T(8,128)(2,1)} %param.8) | copy-start | bytes 1572868
  94.5 117.9 %collective-permute-start.3 = (bf16[1,1024,512]{1,2,0:T(8,128)(2,1)S(1)}, bf16[1,1024,512]{1,2,0:T(8,128)(2,1)S(1)}, u32[]{:S(2)}, u32[]{:S(2)}) collective-permute-start(bf16[1,1024,512]{1,2,0:T(8,128)(2,1)S(1)} %pad_maximum_fusion.3), channel_id=1, source_target_pairs={{8,0},{9,1},{10,2},{11,3},{12,4},{13,5},{14,6},{15,7},{16,8},{17,9... | collective-permute-start | bytes 3145736 | tf_op jit(solution)/shard_map/ppermute | solution.py:10
Sparse Core Ops, SparseCore 0:
  93.4 545.9 all-reduce.4
where the time goes:
time: 649 us
  waiting for transfers between devices  566 us (87%)
  starting transfers between devices  47.2 us (7%)
  between operations  14.4 us (2%)
  matrix products  11.5 us (2%)
  local copies, waits for them, and re-layouts  7.11 us (1%)
    unnamed x2, waiting for transfers between devices  426 us
    ppermute x4, waiting for transfers between devices, from_behind(): return lax.ppermute(block, axis, route)  141 us
    ppermute x4, starting transfers between devices, from_behind(): return lax.ppermute(block, axis, route)  47.1 us
  transfers between devices with their start and end apart: 5, of which 5 were waited for; matrix products, arithmetic and copies ran while one was open for 1% of the time, Pallas kernels for 0%

commit v1 on v0

v1 whole, which is shorter than its diff:
```python
import jax
import jax.numpy as jnp
from jax import lax
from jax.sharding import Mesh
from jax.sharding import PartitionSpec as P

CHUNKS = 1


def split_axes(mesh):
    blocks = mesh.devices.shape[1]
    member = min(32, blocks // 2)
    split = mesh.devices.reshape(mesh.devices.shape[0], blocks // member, member)
    return Mesh(split, ("dp", "group", "member"))


def from_behind(block, distance):
    devices = range(lax.axis_size("group") * lax.axis_size("member"))
    route = [(i - distance, i) for i in devices if i - distance in devices]
    return lax.ppermute(block, ("group", "member"), route)


def contract_rows(left, right):
    return lax.dot_general(
        left, right, (((0,), (0,)), ((), ())), preferred_element_type=jnp.float32
    )


def contract_cols(left, right):
    return lax.dot_general(
        left, right, (((1,), (1,)), ((), ())), preferred_element_type=jnp.float32
    )


def gates(current, earlier, conv_weight):
    pre = jnp.dot(earlier, conv_weight[0], preferred_element_type=jnp.float32) + jnp.dot(
        current, conv_weight[1], preferred_element_type=jnp.float32
    )
    half_width = pre.shape[1] // 2
    return jnp.tanh(pre[:, :half_width]), jax.nn.sigmoid(pre[:, half_width:])


def gate_gradient(tanh_part, sig_part, out_weight, grad_out):
    grad_gated = contract_cols(grad_out, out_weight)
    return jnp.concatenate(
        [
            grad_gated * sig_part * (1.0 - tanh_part * tanh_part),
            grad_gated * tanh_part * sig_part * (1.0 - sig_part),
        ],
        axis=1,
    ).astype(jnp.bfloat16)


def sum_first_stage(terms, scale):
    parts = lax.axis_size("dp") * lax.axis_size("group")
    sent = (terms * scale).astype(jnp.bfloat16).reshape(parts, lax.axis_size("member"), -1)
    received = lax.all_to_all(sent, ("dp", "group"), 0, 0, tiled=True)
    return jnp.sum(received.astype(jnp.float32), axis=0)


def per_device(x, cotangent, conv_first, proj_first, conv_second, proj_second):
    shape = x.shape
    channels = shape[2]
    rows = shape[0] * shape[1]
    blocks = lax.axis_size("group") * lax.axis_size("member")
    near = min(8, blocks // 16)
    far = min(32, blocks // 4)
    scale = float(rows * lax.axis_size("dp") * blocks) ** (-0.5)
    step = rows // CHUNKS

    def pieces(array):
        array = array.reshape(rows, -1)
        return [array[k * step : (k + 1) * step] for k in range(CHUNKS)]

    x, cot = pieces(x), pieces(cotangent)
    past = [from_behind(part, near) for part in x]
    cot_ahead = pieces(from_behind(cotangent.reshape(rows, channels), -far))
    first, middle, middle_past, middle_ahead = [], [], [], []
    for part, earlier in zip(x, past):
        t, s = gates(part, earlier, conv_first)
        gated = (t * s).astype(jnp.bfloat16)
        mid = (
            part.astype(jnp.float32)
            + jnp.dot(gated, proj_first, preferred_element_type=jnp.float32)
        ).astype(jnp.bfloat16)
        first.append((t, s, gated))
        middle.append(mid)
        middle_past.append(from_behind(mid, far))
        middle_ahead.append(from_behind(mid, -far))
    gated_second, grad_pre_first, grad_pre_second, grad_middle, direct, tap_back = (
        [],
        [],
        [],
        [],
        [],
        [],
    )
    for k in range(CHUNKS):
        t, s = gates(middle_ahead[k], middle[k], conv_second)
        ahead = gate_gradient(t, s, proj_second, cot_ahead[k])
        back = contract_cols(ahead, conv_second[0]).astype(jnp.bfloat16)
        t, s = gates(middle[k], middle_past[k], conv_second)
        gated_second.append((t * s).astype(jnp.bfloat16))
        here = gate_gradient(t, s, proj_second, cot[k])
        grad_pre_second.append(here)
        grad = (
            cot[k].astype(jnp.float32)
            + contract_cols(here, conv_second[1])
            + back.astype(jnp.float32)
        ).astype(jnp.bfloat16)
        grad_middle.append(grad)
        t, s, _ = first[k]
        here = gate_gradient(t, s, proj_first, grad)
        grad_pre_first.append(here)
        tap_back.append(
            from_behind(contract_cols(here, conv_first[0]).astype(jnp.bfloat16), -near)
        )
        direct.append(grad.astype(jnp.float32) + contract_cols(here, conv_first[1]))

    def whole(parts):
        return jnp.concatenate(parts, axis=0)

    def weight_gradient(earlier, current, grad_pre, gated, grad_out):
        grad_pre = whole(grad_pre)
        return jnp.concatenate(
            [
                contract_rows(whole(earlier), grad_pre).reshape(-1),
                contract_rows(whole(current), grad_pre).reshape(-1),
                contract_rows(whole(gated), whole(grad_out)).reshape(-1),
            ]
        )

    terms_second = weight_gradient(middle_past, middle, grad_pre_second, gated_second, cot)
    sums_second = sum_first_stage(terms_second, scale)
    terms_first = weight_gradient(past, x, grad_pre_first, [g for _, _, g in first], grad_middle)
    sums_first = sum_first_stage(terms_first, scale)
    sent = jnp.concatenate([sums_first, sums_second], axis=1).astype(jnp.bfloat16)
    received = lax.all_to_all(sent, "member", 0, 0, tiled=True)
    sums = jnp.sum(received.astype(jnp.float32), axis=0)
    length = sums.shape[0] // 2
    grad_x = whole(
        [(d + back.astype(jnp.float32)).astype(jnp.bfloat16) for d, back in zip(direct, tap_back)]
    )
    return grad_x.reshape(shape), sums[:length], sums[length:]


def solution(mesh):
    time, flat = P("dp", ("group", "member"), None), P(("dp", "group", "member"))
    return jax.shard_map(
        per_device,
        mesh=split_axes(mesh),
        in_specs=(time, time, P(), P(), P(), P()),
        out_specs=(time, flat, flat),
        check_vma=False,
    )
```

time: 649 us -> 164 us (0.25)
  waiting for transfers between devices: 566 us -> 57.3 us
  starting transfers between devices: 47.2 us -> 81.2 us
  between operations: 14.4 us -> 1.14 us
    unnamed x2 -> x0, waiting for transfers between devices: 426 us -> none
    ppermute x4 -> x5, waiting for transfers between devices: 141 us -> 37.7 us  [from_behind(): return lax.ppermute(block, ('group', 'member'), route)]
    all_to_all x0 -> x3, starting transfers between devices: none -> 26.6 us  [the longest x2 14.3 us: sum_first_stage(): received = lax.all_to_all(sent, ('dp', 'group'), 0, 0, tiled=True)]
    all_to_all x0 -> x3, waiting for transfers between devices: none -> 19.6 us  [the longest x1 12.7 us: per_device(): received = lax.all_to_all(sent, 'member', 0, 0, tiled=True)]
    ppermute x4 -> x5, starting transfers between devices: 47.1 us -> 54.5 us  [from_behind(): return lax.ppermute(block, ('group', 'member'), route)]
  transfers between devices with their start and end apart: 5 -> 8, of which waited for: 5 -> 6; matrix products, arithmetic and copies ran while one was open for 1% -> 8% of each run, Pallas kernels for 0% -> 0%
where the time goes in v1:
time: 164 us; the launch traced here: 163 us
  starting transfers between devices  81.2 us (50%)
  waiting for transfers between devices  57.3 us (35%)
  matrix products  14.7 us (9%)
  local copies, waits for them, and re-layouts  7.12 us (4%)
  other arithmetic  1.66 us (1%)
    ppermute x5, starting transfers between devices, from_behind(): return lax.ppermute(block, ('group', 'member'), route)  54.5 us
    ppermute x5, waiting for transfers between devices, from_behind(): return lax.ppermute(block, ('group', 'member'), route)  37.7 us
    all_to_all x2, starting transfers between devices, sum_first_stage(): received = lax.all_to_all(sent, ('dp', 'group'), 0, 0, tiled=True)  14.3 us
    all_to_all x1, waiting for transfers between devices, per_device(): received = lax.all_to_all(sent, 'member', 0, 0, tiled=True)  12.7 us
    all_to_all x1, starting transfers between devices, per_device(): received = lax.all_to_all(sent, 'member', 0, 0, tiled=True)  12.3 us
    dot_general x7, matrix products, contract_cols(): lax.dot_general(left, right, (((1,), (1,)), ((), ())), preferred_element_...  6.87 us
    all_to_all x2, waiting for transfers between devices, sum_first_stage(): received = lax.all_to_all(sent, ('dp', 'group'), 0, 0, tiled=True)  6.84 us
    dot_general x6, matrix products, contract_rows(): lax.dot_general(left, right, (((0,), (0,)), ((), ())), preferred_element_...  3.5 us
  transfers between devices with their start and end apart: 8, of which 6 were waited for; matrix products, arithmetic and copies ran while one was open for 8% of the time, Pallas kernels for 0%

profile of v1, /device:TPU:6, one launch (start us, length us, event | category | flops | bytes accessed | tf_op | source)
XLA Modules:
  0.0 163.1 jit_solution(6825691993850114802)
XLA Ops:
  0.6 0.0 copy-start
  0.6 0.0 copy-start.4
  0.7 9.2 %collective-permute-start = (bf16[1024,256]{1,0:T(8,128)(2,1)}, bf16[1024,256]{1,0:T(8,128)(2,1)S(1)}, u32[]{:S(2)}, u32[]{:S(2)}) collective-permute-start(bf16[1024,256]{1,0:T(8,128)(2,1)} %bitcast.81), channel_id=1, source_target_pairs={{0,8},{1,9},{2,10},{3,11},{4,12},{5,13},{6,14},{7,15},{8,16},{9,17... | collective-permute-start | bytes 1572872 | tf_op jit(solution)/shard_map/ppermute | solution.py:20
  9.9 2.7 %collective-permute-start.2 = (bf16[1024,256]{1,0:T(8,128)(2,1)}, bf16[1024,256]{1,0:T(8,128)(2,1)S(1)}, u32[]{:S(2)}, u32[]{:S(2)}) collective-permute-start(bf16[1024,256]{1,0:T(8,128)(2,1)} %bitcast.90), channel_id=1, source_target_pairs={{32,0},{33,1},{34,2},{35,3},{36,4},{37,5},{38,6},{39,7},{40,8},{41... | collective-permute-start | bytes 1572872 | tf_op jit(solution)/shard_map/ppermute | solution.py:20
  12.6 1.6 fusion.28
  14.2 20.7 %collective-permute-done = bf16[1024,256]{1,0:T(8,128)(2,1)S(1)} collective-permute-done((bf16[1024,256]{1,0:T(8,128)(2,1)}, bf16[1024,256]{1,0:T(8,128)(2,1)S(1)}, u32[]{:S(2)}, u32[]{:S(2)}) %collective-permute-start) | collective-permute-done | bytes 524320 | tf_op jit(solution)/shard_map/ppermute | solution.py:20
  35.0 0.5 convolution_add_fusion.2
  35.5 0.0 copy-start.2
  35.5 0.4 multiply_convert_fusion.7
  35.9 0.6 copy-done.1
  36.5 0.0 copy-done.6
  36.5 0.4 fusion.5
  36.9 2.4 %collective-permute-start.3 = (bf16[1024,256]{1,0:T(8,128)(2,1)S(1)}, bf16[1024,256]{1,0:T(8,128)(2,1)S(1)}, u32[]{:S(2)}, u32[]{:S(2)}) collective-permute-start(bf16[1024,256]{1,0:T(8,128)(2,1)S(1)} %fusion.5), channel_id=1, source_target_pairs={{32,0},{33,1},{34,2},{35,3},{36,4},{37,5},{38,6},{39,7},{40,8},{41... | collective-permute-start | bytes 1572872 | tf_op jit(solution)/shard_map/ppermute | solution.py:20
  39.4 7.0 %collective-permute-start.1 = (bf16[1024,256]{1,0:T(8,128)(2,1)S(1)}, bf16[1024,256]{1,0:T(8,128)(2,1)S(1)}, u32[]{:S(2)}, u32[]{:S(2)}) collective-permute-start(bf16[1024,256]{1,0:T(8,128)(2,1)S(1)} %fusion.5), channel_id=1, source_target_pairs={{0,32},{1,33},{2,34},{3,35},{4,36},{5,37},{6,38},{7,39},{8,40},{9,... | collective-permute-start | bytes 1572872 | tf_op jit(solution)/shard_map/ppermute | solution.py:20
  46.4 0.5 fusion.24
  46.9 0.5 fusion.21
  47.4 5.6 %collective-permute-done.3 = bf16[1024,256]{1,0:T(8,128)(2,1)S(1)} collective-permute-done((bf16[1024,256]{1,0:T(8,128)(2,1)S(1)}, bf16[1024,256]{1,0:T(8,128)(2,1)S(1)}, u32[]{:S(2)}, u32[]{:S(2)}) %collective-permute-start.3) | collective-permute-done | bytes 524320 | tf_op jit(solution)/shard_map/ppermute | solution.py:20
  53.0 0.5 convolution_add_fusion
  53.5 0.7 collective-permute-done.1
  54.1 0.5 convolution_add_fusion.1
  54.7 0.5 convolution_bitcast_fusion.4
  55.2 0.7 multiply_convert_fusion.6
  56.0 0.7 multiply_convert_fusion.4
  56.7 0.5 fusion.3
  57.2 0.5 fusion.4
  57.7 0.7 multiply_convert_fusion.2
  58.4 0.3 convolution_bitcast_fusion.5
  58.7 0.5 convolution_bitcast_fusion
  59.2 1.3 convolution_bitcast_fusion.2
  60.5 0.4 convolution_bitcast_fusion.3
  60.9 0.2 copy.16
  61.1 0.0 copy-start.11
  61.2 0.1 copy.19
  61.3 0.1 copy.21
  61.4 0.1 copy.23
  61.6 0.6 copy-done.9
  62.2 0.2 copy-done.11
  62.3 0.5 convolution_bitcast_fusion.1
  62.8 0.1 copy.22
  63.0 0.1 copy.24
  63.1 0.1 fusion.2
  63.2 1.3 convert_element_type.87
  64.6 8.7 %all-to-all-start.1 = ((bf16[16,32,640]{2,1,0:T(8,128)(2,1)}), bf16[16,32,640]{2,1,0:T(8,128)(2,1)S(1)}, u32[]{:S(2)}, u32[]{:S(2)}) async-start(bf16[16,32,640]{2,1,0:T(8,128)(2,1)} %convert_element_type.87), calls=%async_computation.1 | async-start | bytes 1310720 | tf_op jit(solution)/shard_map/all_to_all | solution.py:57
  73.2 0.2 copy.17
  73.4 0.1 copy.20
  73.6 0.1 fusion.1
  73.7 0.0 copy-start.5
  73.7 1.3 convert_element_type.83
  75.0 6.8 %all-to-all-done.1 = bf16[16,32,640]{2,1,0:T(8,128)(2,1)S(1)} async-done(((bf16[16,32,640]{2,1,0:T(8,128)(2,1)}), bf16[16,32,640]{2,1,0:T(8,128)(2,1)S(1)}, u32[]{:S(2)}, u32[]{:S(2)}) %all-to-all-start.1) | async-done | bytes 655392 | tf_op jit(solution)/shard_map/all_to_all | solution.py:57
  81.9 5.7 %all-to-all-start = ((bf16[16,32,640]{2,1,0:T(8,128)(2,1)}), bf16[16,32,640]{2,1,0:T(8,128)(2,1)S(1)}, u32[]{:S(2)}, u32[]{:S(2)}) async-start(bf16[16,32,640]{2,1,0:T(8,128)(2,1)} %convert_element_type.83), calls=%async_computation | async-start | bytes 1310720 | tf_op jit(solution)/shard_map/all_to_all | solution.py:57
  87.6 1.3 convolution_convert_fusion
  88.9 33.1 %collective-permute-start.4 = (bf16[1024,256]{1,0:T(8,128)(2,1)}, bf16[1024,256]{1,0:T(8,128)(2,1)S(1)}, u32[]{:S(2)}, u32[]{:S(2)}) collective-permute-start(bf16[1024,256]{1,0:T(8,128)(2,1)} %convolution_convert_fusion), channel_id=1, source_target_pairs={{8,0},{9,1},{10,2},{11,3},{12,4},{13,5},{14,6},{15,7},{16,8},{17,9... | collective-permute-start | bytes 1572872 | tf_op jit(solution)/shard_map/ppermute | solution.py:20
  122.0 0.1 reduce.2
  122.1 0.1 reduce.1
  122.2 0.5 broadcast.41
  122.7 0.7 reduce.3
  123.4 0.7 reshape.87
  124.0 12.3 %all-to-all-start.2 = ((bf16[32,2,640]{2,1,0:T(2,128)(2,1)}), bf16[32,2,640]{2,1,0:T(2,128)(2,1)S(1)}, u32[]{:S(2)}, u32[]{:S(2)}) async-start(bf16[32,2,640]{2,1,0:T(2,128)(2,1)} %reshape.87), calls=%async_computation.2 | async-start | bytes 163840 | tf_op jit(solution)/shard_map/all_to_all | solution.py:138
  136.4 10.7 %collective-permute-done.4 = bf16[1024,256]{1,0:T(8,128)(2,1)S(1)} collective-permute-done((bf16[1024,256]{1,0:T(8,128)(2,1)}, bf16[1024,256]{1,0:T(8,128)(2,1)S(1)}, u32[]{:S(2)}, u32[]{:S(2)}) %collective-permute-start.4) | collective-permute-done | bytes 524320 | tf_op jit(solution)/shard_map/ppermute | solution.py:20
  147.1 2.5 %fusion.18 = bf16[1,1024,256]{2,1,0:T(8,128)(2,1)} fusion(bf16[1024,256]{1,0:T(8,128)(2,1)S(1)} %collective-permute-done.4, bf16[1024,256]{1,0:T(8,128)(2,1)S(1)} %fusion.4, bf16[2,256,512]{2,1,0:T(8,128)(2,1)S(1)} %copy-done.5, bf16[1024,256]{0,1:T(8,128)(2,1)} %copy-done.14, bf16[1024,256]{0,1:T(8,128)(2,1)} %copy-done.12), kind=kOutput, calls=%fused_computation.46 | convolution fusion | flops 271843328 | bytes 2883584 | tf_op jit(solution)/shard_map/dot_general | solution.py:30
  149.5 12.7 %all-to-all-done.2 = bf16[32,2,640]{2,1,0:T(2,128)(2,1)S(1)} async-done(((bf16[32,2,640]{2,1,0:T(2,128)(2,1)}), bf16[32,2,640]{2,1,0:T(2,128)(2,1)S(1)}, u32[]{:S(2)}, u32[]{:S(2)}) %all-to-all-start.2) | async-done | bytes 81952 | tf_op jit(solution)/shard_map/all_to_all | solution.py:138
  162.2 0.1 reshape.88
  162.3 0.2 convert_reduce_fusion
  162.5 0.6 fusion.52
  (26 shorter events, 0.1 us)
Async XLA Ops:
  0.6 54.6 %copy-start = (bf16[256,256]{1,0:T(8,128)(2,1)S(1)}, bf16[256,256]{1,0:T(8,128)(2,1)}, u32[]{:S(2)}) copy-start(bf16[256,256]{1,0:T(8,128)(2,1)} %param.11) | copy-start | bytes 393220
  0.6 34.3 %copy-start.4 = (bf16[2,256,512]{2,1,0:T(8,128)(2,1)S(1)}, bf16[2,256,512]{2,1,0:T(8,128)(2,1)}, u32[]{:S(2)}) copy-start(bf16[2,256,512]{2,1,0:T(8,128)(2,1)} %param.8) | copy-start | bytes 1572868
  0.7 34.3 %collective-permute-start = (bf16[1024,256]{1,0:T(8,128)(2,1)}, bf16[1024,256]{1,0:T(8,128)(2,1)S(1)}, u32[]{:S(2)}, u32[]{:S(2)}) collective-permute-start(bf16[1024,256]{1,0:T(8,128)(2,1)} %bitcast.81), channel_id=1, source_target_pairs={{0,8},{1,9},{2,10},{3,11},{4,12},{5,13},{6,14},{7,15},{8,16},{9,17... | collective-permute-start | bytes 1572872 | tf_op jit(solution)/shard_map/ppermute | solution.py:20
  9.9 46.1 %collective-permute-start.2 = (bf16[1024,256]{1,0:T(8,128)(2,1)}, bf16[1024,256]{1,0:T(8,128)(2,1)S(1)}, u32[]{:S(2)}, u32[]{:S(2)}) collective-permute-start(bf16[1024,256]{1,0:T(8,128)(2,1)} %bitcast.90), channel_id=1, source_target_pairs={{32,0},{33,1},{34,2},{35,3},{36,4},{37,5},{38,6},{39,7},{40,8},{41... | collective-permute-start | bytes 1572872 | tf_op jit(solution)/shard_map/ppermute | solution.py:20
  35.5 1.0 copy-start.1
  35.5 1.1 copy-start.6
  35.5 10.9 %copy-start.2 = (bf16[2,256,512]{2,1,0:T(8,128)(2,1)S(1)}, bf16[2,256,512]{2,1,0:T(8,128)(2,1)}, u32[]{:S(2)}) copy-start(bf16[2,256,512]{2,1,0:T(8,128)(2,1)} %param.10) | copy-start | bytes 1572868
  36.9 16.1 %collective-permute-start.3 = (bf16[1024,256]{1,0:T(8,128)(2,1)S(1)}, bf16[1024,256]{1,0:T(8,128)(2,1)S(1)}, u32[]{:S(2)}, u32[]{:S(2)}) collective-permute-start(bf16[1024,256]{1,0:T(8,128)(2,1)S(1)} %fusion.5), channel_id=1, source_target_pairs={{32,0},{33,1},{34,2},{35,3},{36,4},{37,5},{38,6},{39,7},{40,8},{41... | collective-permute-start | bytes 1572872 | tf_op jit(solution)/shard_map/ppermute | solution.py:20
  39.4 14.8 %collective-permute-start.1 = (bf16[1024,256]{1,0:T(8,128)(2,1)S(1)}, bf16[1024,256]{1,0:T(8,128)(2,1)S(1)}, u32[]{:S(2)}, u32[]{:S(2)}) collective-permute-start(bf16[1024,256]{1,0:T(8,128)(2,1)S(1)} %fusion.5), channel_id=1, source_target_pairs={{0,32},{1,33},{2,34},{3,35},{4,36},{5,37},{6,38},{7,39},{8,40},{9,... | collective-permute-start | bytes 1572872 | tf_op jit(solution)/shard_map/ppermute | solution.py:20
  53.5 1.2 copy-start.7
  55.9 2.8 %copy-start.8 = (bf16[1024,256]{0,1:T(8,128)(2,1)}, bf16[1024,256]{0,1:T(8,128)(2,1)S(1)}, u32[]{:S(2)}) copy-start(bf16[1024,256]{0,1:T(8,128)(2,1)S(1)} %get-tuple-element.5) | copy-start | bytes 1572868
  55.9 2.8 %copy-start.10 = (bf16[1024,256]{0,1:T(8,128)(2,1)}, bf16[1024,256]{0,1:T(8,128)(2,1)S(1)}, u32[]{:S(2)}) copy-start(bf16[1024,256]{0,1:T(8,128)(2,1)S(1)} %get-tuple-element.6) | copy-start | bytes 1572868
  58.4 2.1 %copy-start.12 = (bf16[1024,256]{0,1:T(8,128)(2,1)}, bf16[1024,256]{0,1:T(8,128)(2,1)S(1)}, u32[]{:S(2)}) copy-start(bf16[1024,256]{0,1:T(8,128)(2,1)S(1)} %get-tuple-element.3) | copy-start | bytes 1572868
  58.4 2.1 %copy-start.14 = (bf16[1024,256]{0,1:T(8,128)(2,1)}, bf16[1024,256]{0,1:T(8,128)(2,1)S(1)}, u32[]{:S(2)}) copy-start(bf16[1024,256]{0,1:T(8,128)(2,1)S(1)} %get-tuple-element.4) | copy-start | bytes 1572868
  61.1 1.0 copy-start.9
  61.1 1.2 copy-start.11
  63.1 10.1 %copy-start.3 = (f32[256,512]{0,1:T(8,128)S(1)}, f32[256,512]{0,1:T(8,128)}, u32[]{:S(2)}) copy-start(f32[256,512]{0,1:T(8,128)} %convolution_bitcast_fusion.2) | copy-start | bytes 1572868
  64.6 17.3 %all-to-all-start.1 = ((bf16[16,32,640]{2,1,0:T(8,128)(2,1)}), bf16[16,32,640]{2,1,0:T(8,128)(2,1)S(1)}, u32[]{:S(2)}, u32[]{:S(2)}) async-start(bf16[16,32,640]{2,1,0:T(8,128)(2,1)} %convert_element_type.87), calls=%async_computation.1 | async-start | bytes 1310720 | tf_op jit(solution)/shard_map/all_to_all | solution.py:57
  73.7 13.9 %copy-start.5 = (bf16[2,256,512]{2,1,0:T(8,128)(2,1)S(1)}, bf16[2,256,512]{2,1,0:T(8,128)(2,1)}, u32[]{:S(2)}) copy-start(bf16[2,256,512]{2,1,0:T(8,128)(2,1)} %param.8) | copy-start | bytes 1572868
  73.7 13.9 %copy-start.13 = (bf16[1024,256]{0,1:T(8,128)(2,1)S(1)}, bf16[1024,256]{0,1:T(8,128)(2,1)}, u32[]{:S(2)}) copy-start(bf16[1024,256]{0,1:T(8,128)(2,1)} %copy-done.12) | copy-start | bytes 1572868
  73.7 13.9 %copy-start.15 = (bf16[1024,256]{0,1:T(8,128)(2,1)S(1)}, bf16[1024,256]{0,1:T(8,128)(2,1)}, u32[]{:S(2)}) copy-start(bf16[1024,256]{0,1:T(8,128)(2,1)} %copy-done.14) | copy-start | bytes 1572868
  81.9 40.2 %all-to-all-start = ((bf16[16,32,640]{2,1,0:T(8,128)(2,1)}), bf16[16,32,640]{2,1,0:T(8,128)(2,1)S(1)}, u32[]{:S(2)}, u32[]{:S(2)}) async-start(bf16[16,32,640]{2,1,0:T(8,128)(2,1)} %convert_element_type.83), calls=%async_computation | async-start | bytes 1310720 | tf_op jit(solution)/shard_map/all_to_all | solution.py:57
  88.9 58.2 %collective-permute-start.4 = (bf16[1024,256]{1,0:T(8,128)(2,1)}, bf16[1024,256]{1,0:T(8,128)(2,1)S(1)}, u32[]{:S(2)}, u32[]{:S(2)}) collective-permute-start(bf16[1024,256]{1,0:T(8,128)(2,1)} %convolution_convert_fusion), channel_id=1, source_target_pairs={{8,0},{9,1},{10,2},{11,3},{12,4},{13,5},{14,6},{15,7},{16,8},{17,9... | collective-permute-start | bytes 1572872 | tf_op jit(solution)/shard_map/ppermute | solution.py:20
  124.0 38.2 %all-to-all-start.2 = ((bf16[32,2,640]{2,1,0:T(2,128)(2,1)}), bf16[32,2,640]{2,1,0:T(2,128)(2,1)S(1)}, u32[]{:S(2)}, u32[]{:S(2)}) async-start(bf16[32,2,640]{2,1,0:T(2,128)(2,1)} %reshape.87), calls=%async_computation.2 | async-start | bytes 163840 | tf_op jit(solution)/shard_map/all_to_all | solution.py:138

commit v2 on v1

v2 whole, which is shorter than its diff:
```python
import jax
import jax.numpy as jnp
from jax import lax
from jax.sharding import Mesh
from jax.sharding import PartitionSpec as P

CHUNKS = (0, 384, 768, 1024)


def split_axes(mesh):
    blocks = mesh.devices.shape[1]
    member = min(32, blocks // 2)
    split = mesh.devices.reshape(mesh.devices.shape[0], blocks // member, member)
    return Mesh(split, ("dp", "group", "member"))


def from_behind(block, distance):
    devices = range(lax.axis_size("group") * lax.axis_size("member"))
    route = [(i - distance, i) for i in devices if i - distance in devices]
    return lax.ppermute(block, ("group", "member"), route)


def contract_rows(left, right):
    return lax.dot_general(
        left, right, (((0,), (0,)), ((), ())), preferred_element_type=jnp.float32
    )


def contract_cols(left, right):
    return lax.dot_general(
        left, right, (((1,), (1,)), ((), ())), preferred_element_type=jnp.float32
    )


def gates(current, earlier, conv_weight):
    pre = jnp.dot(earlier, conv_weight[0], preferred_element_type=jnp.float32) + jnp.dot(
        current, conv_weight[1], preferred_element_type=jnp.float32
    )
    return halves(pre)


def halves(pre):
    half_width = pre.shape[1] // 2
    return jnp.tanh(pre[:, :half_width]), jax.nn.sigmoid(pre[:, half_width:])


def gate_gradient(tanh_part, sig_part, out_weight, grad_out):
    grad_gated = contract_cols(grad_out, out_weight)
    return jnp.concatenate(
        [
            grad_gated * sig_part * (1.0 - tanh_part * tanh_part),
            grad_gated * tanh_part * sig_part * (1.0 - sig_part),
        ],
        axis=1,
    ).astype(jnp.bfloat16)


def pack(terms_first, terms_second, scale):
    parts = lax.axis_size("dp") * lax.axis_size("group")
    members = lax.axis_size("member")
    return jnp.concatenate(
        [
            (terms * scale).astype(jnp.bfloat16).reshape(parts, members, -1)
            for terms in (terms_first, terms_second)
        ],
        axis=2,
    )


def per_device(x, cotangent, conv_first, proj_first, conv_second, proj_second):
    shape = x.shape
    channels = shape[2]
    rows = shape[0] * shape[1]
    blocks = lax.axis_size("group") * lax.axis_size("member")
    near = min(8, blocks // 16)
    far = min(32, blocks // 4)
    scale = float(rows * lax.axis_size("dp") * blocks) ** (-0.5)
    edges = [edge * rows // 1024 for edge in CHUNKS]
    last = len(edges) - 2

    def pieces(array):
        array = array.reshape(rows, -1)
        return [array[start:end] for start, end in zip(edges, edges[1:])]

    x, cot = pieces(x), pieces(cotangent)
    own, past = [], []
    sent = x[0]
    for k in range(last + 1):
        past.append(from_behind(sent, near))
        own.append(jnp.dot(x[k], conv_first[1], preferred_element_type=jnp.float32))
        following = x[k + 1] if k < last else cotangent
        own[k], sent = lax.optimization_barrier((own[k], following))
    cot_ahead = pieces(from_behind(sent.reshape(rows, channels), -far))
    first, middle, middle_past, middle_ahead = [], [], [], []
    for k in range(last + 1):
        if k:
            past[k], middle_past[k - 1], middle_ahead[k - 1] = lax.optimization_barrier(
                (past[k], middle_past[k - 1], middle_ahead[k - 1])
            )
        t, s = halves(
            own[k] + jnp.dot(past[k], conv_first[0], preferred_element_type=jnp.float32)
        )
        gated = (t * s).astype(jnp.bfloat16)
        mid = (
            x[k].astype(jnp.float32)
            + jnp.dot(gated, proj_first, preferred_element_type=jnp.float32)
        ).astype(jnp.bfloat16)
        first.append((t, s, gated))
        middle.append(mid)
        middle_past.append(from_behind(mid, far))
        middle_ahead.append(from_behind(mid, -far))
    direct, tap_back = [], []
    totals = None
    for k in range(last + 1):
        t, s = gates(middle_ahead[k], middle[k], conv_second)
        ahead = gate_gradient(t, s, proj_second, cot_ahead[k])
        back = contract_cols(ahead, conv_second[0]).astype(jnp.bfloat16)
        t, s = gates(middle[k], middle_past[k], conv_second)
        gated_second = (t * s).astype(jnp.bfloat16)
        grad_pre_second = gate_gradient(t, s, proj_second, cot[k])
        grad = (
            cot[k].astype(jnp.float32)
            + contract_cols(grad_pre_second, conv_second[1])
            + back.astype(jnp.float32)
        ).astype(jnp.bfloat16)
        t, s, gated = first[k]
        grad_pre = gate_gradient(t, s, proj_first, grad)
        tap = contract_cols(grad_pre, conv_first[0]).astype(jnp.bfloat16)
        tap_back.append(from_behind(tap, -near))
        direct.append(grad.astype(jnp.float32) + contract_cols(grad_pre, conv_first[1]))
        terms = [
            contract_rows(past[k], grad_pre),
            contract_rows(x[k], grad_pre),
            contract_rows(gated, grad),
            contract_rows(middle_past[k], grad_pre_second),
            contract_rows(middle[k], grad_pre_second),
            contract_rows(gated_second, cot[k]),
        ]
        totals = terms if totals is None else [a + b for a, b in zip(totals, terms)]
    totals = [total.reshape(-1) for total in totals]
    sent = pack(jnp.concatenate(totals[:3]), jnp.concatenate(totals[3:]), scale)
    early = lax.optimization_barrier((sent, *tap_back[:last]))
    tap_back[:last] = early[1:]
    received = lax.all_to_all(early[0], ("dp", "group"), 0, 0, tiled=True)
    sent = jnp.sum(received.astype(jnp.float32), axis=0).astype(jnp.bfloat16)
    received = lax.all_to_all(sent, "member", 0, 0, tiled=True)
    sums = jnp.sum(received.astype(jnp.float32), axis=0)
    length = sums.shape[0] // 2
    grad_x = jnp.concatenate(
        [(d + back.astype(jnp.float32)).astype(jnp.bfloat16) for d, back in zip(direct, tap_back)]
    )
    return grad_x.reshape(shape), sums[:length], sums[length:]


def solution(mesh):
    time, flat = P("dp", ("group", "member"), None), P(("dp", "group", "member"))
    return jax.shard_map(
        per_device,
        mesh=split_axes(mesh),
        in_specs=(time, time, P(), P(), P(), P()),
        out_specs=(time, flat, flat),
        check_vma=False,
    )
```

time: 164 us -> 203 us (1.24); the launches traced: 163 us -> 200 us
  matrix products: 14.7 us -> 40.8 us
  waiting for transfers between devices: 57.3 us -> 65.6 us
  starting transfers between devices: 81.2 us -> 74.6 us
  other arithmetic: 1.66 us -> 5.83 us
  local copies, waits for them, and re-layouts: 7.12 us -> 11.1 us
    dot_general x6 -> x18, matrix products: 3.5 us -> 13.5 us  [contract_rows(): lax.dot_general(left, right, (((0,), (0,)), ((), ())), preferred_element_...]
    dot_general x7 -> x21, matrix products: 6.87 us -> 16.8 us  [contract_cols(): lax.dot_general(left, right, (((1,), (1,)), ((), ())), preferred_element_...]
    dot_general x0 -> x6, matrix products: none -> 6.22 us  [the longest x3 3.64 us: per_device(): jnp.dot(past[k], conv_first[0], preferred_element_type=jnp.float32)]
    all_to_all x1, starting transfers between devices: 12.3 us -> 6.79 us  [per_device(): received = lax.all_to_all(sent, 'member', 0, 0, tiled=True)]
    ppermute x5 -> x13, waiting for transfers between devices: 37.7 us -> 41.4 us  [from_behind(): return lax.ppermute(block, ('group', 'member'), route)]
    all_to_all x2 -> x1, waiting for transfers between devices: 6.84 us -> 10.2 us  [per_device(): received = lax.all_to_all(early[0], ('dp', 'group'), 0, 0, tiled=True)]
    all_to_all x2 -> x1, starting transfers between devices: 14.3 us -> 11.2 us  [per_device(): received = lax.all_to_all(early[0], ('dp', 'group'), 0, 0, tiled=True)]
    slice x0 -> x2, local copies, waits for them, and re-layouts: none -> 2.45 us  [pieces(): return [array[start:end] for start, end in zip(edges, edges[1:])]]
  transfers between devices with their start and end apart: 8 -> 15, of which waited for: 6 -> 5; matrix products, arithmetic and copies ran while one was open for 8% -> 26% of each run, Pallas kernels for 0% -> 0%
where the time goes in v2:
time: 203 us; the launch traced here: 200 us
  starting transfers between devices  74.6 us (37%)
  waiting for transfers between devices  65.6 us (32%)
  matrix products  40.8 us (20%)
  local copies, waits for them, and re-layouts  11.1 us (5%)
  other arithmetic  5.83 us (3%)
    ppermute x13, starting transfers between devices, from_behind(): return lax.ppermute(block, ('group', 'member'), route)  56.6 us
    ppermute x13, waiting for transfers between devices, from_behind(): return lax.ppermute(block, ('group', 'member'), route)  41.4 us
    dot_general x21, matrix products, contract_cols(): lax.dot_general(left, right, (((1,), (1,)), ((), ())), preferred_element_...  16.8 us
    all_to_all x1, waiting for transfers between devices, per_device(): received = lax.all_to_all(sent, 'member', 0, 0, tiled=True)  14 us
    dot_general x18, matrix products, contract_rows(): lax.dot_general(left, right, (((0,), (0,)), ((), ())), preferred_element_...  13.5 us
    all_to_all x1, starting transfers between devices, per_device(): received = lax.all_to_all(early[0], ('dp', 'group'), 0, 0, tiled=True)  11.2 us
    all_to_all x1, waiting for transfers between devices, per_device(): received = lax.all_to_all(early[0], ('dp', 'group'), 0, 0, tiled=True)  10.2 us
    all_to_all x1, starting transfers between devices, per_device(): received = lax.all_to_all(sent, 'member', 0, 0, tiled=True)  6.79 us
  transfers between devices with their start and end apart: 15, of which 5 were waited for; matrix products, arithmetic and copies ran while one was open for 26% of the time, Pallas kernels for 0%

profile of v2, /device:TPU:6, one launch (start us, length us, event | category | flops | bytes accessed | tf_op | source)
XLA Modules:
  0.0 199.6 jit_solution(10988543245896141243)
XLA Ops:
  0.7 1.7 slice_bitcast_fusion.2
  2.3 1.3 fusion.90
  3.6 9.1 %collective-permute-start.5 = (bf16[256,256]{1,0:T(8,128)(2,1)}, bf16[256,256]{1,0:T(8,128)(2,1)}, u32[]{:S(2)}, u32[]{:S(2)}) collective-permute-start(bf16[256,256]{1,0:T(8,128)(2,1)} %slice_bitcast_fusion.2), channel_id=1, source_target_pairs={{0,8},{1,9},{2,10},{3,11},{4,12},{5,13},{6,14},{7,15},{8,16},{9,17... | collective-permute-start | bytes 393224 | tf_op jit(solution)/shard_map/ppermute | solution.py:20
  13.0 0.8 slice_bitcast_fusion.1
  13.8 9.1 %collective-permute-start = (bf16[384,256]{1,0:T(8,128)(2,1)}, bf16[384,256]{1,0:T(8,128)(2,1)}, u32[]{:S(2)}, u32[]{:S(2)}) collective-permute-start(bf16[384,256]{1,0:T(8,128)(2,1)} %get-tuple-element.18), channel_id=1, source_target_pairs={{0,8},{1,9},{2,10},{3,11},{4,12},{5,13},{6,14},{7,15},{8,16},{9,17... | collective-permute-start | bytes 589832 | tf_op jit(solution)/shard_map/ppermute | solution.py:20
  22.9 4.3 %collective-permute-start.1 = (bf16[384,256]{1,0:T(8,128)(2,1)}, bf16[384,256]{1,0:T(8,128)(2,1)}, u32[]{:S(2)}, u32[]{:S(2)}) collective-permute-start(bf16[384,256]{1,0:T(8,128)(2,1)} %get-tuple-element.51), channel_id=1, source_target_pairs={{0,8},{1,9},{2,10},{3,11},{4,12},{5,13},{6,14},{7,15},{8,16},{9,17... | collective-permute-start | bytes 589832 | tf_op jit(solution)/shard_map/ppermute | solution.py:20
  27.2 1.0 fusion.93
  28.2 2.7 %collective-permute-start.4 = (bf16[1024,256]{1,0:T(8,128)(2,1)}, bf16[1024,256]{1,0:T(8,128)(2,1)}, u32[]{:S(2)}, u32[]{:S(2)}) collective-permute-start(bf16[1024,256]{1,0:T(8,128)(2,1)} %bitcast.8), channel_id=1, source_target_pairs={{32,0},{33,1},{34,2},{35,3},{36,4},{37,5},{38,6},{39,7},{40,8},{41... | collective-permute-start | bytes 1572872 | tf_op jit(solution)/shard_map/ppermute | solution.py:20
  31.5 32.1 %collective-permute-done.1 = bf16[384,256]{1,0:T(8,128)(2,1)} collective-permute-done((bf16[384,256]{1,0:T(8,128)(2,1)}, bf16[384,256]{1,0:T(8,128)(2,1)}, u32[]{:S(2)}, u32[]{:S(2)}) %collective-permute-start.1) | collective-permute-done | bytes 196640 | tf_op jit(solution)/shard_map/ppermute | solution.py:20
  63.6 1.3 convolution_add_fusion.5
  65.4 8.3 %collective-permute-start.2 = (bf16[384,256]{1,0:T(8,128)(2,1)S(1)}, bf16[384,256]{1,0:T(8,128)(2,1)S(1)}, u32[]{:S(2)}, u32[]{:S(2)}) collective-permute-start(bf16[384,256]{1,0:T(8,128)(2,1)S(1)} %fusion.12), channel_id=1, source_target_pairs={{0,32},{1,33},{2,34},{3,35},{4,36},{5,37},{6,38},{7,39},{8,40},{9,... | collective-permute-start | bytes 589832 | tf_op jit(solution)/shard_map/ppermute | solution.py:20
  73.6 1.9 collective-permute-start.3
  76.3 1.5 collective-permute-done.2
  77.8 7.7 %collective-permute-done.3 = bf16[384,256]{1,0:T(8,128)(2,1)S(1)} collective-permute-done((bf16[384,256]{1,0:T(8,128)(2,1)S(1)}, bf16[384,256]{1,0:T(8,128)(2,1)S(1)}, u32[]{:S(2)}, u32[]{:S(2)}) %collective-permute-start.3) | collective-permute-done | bytes 196640 | tf_op jit(solution)/shard_map/ppermute | solution.py:20
  85.5 1.3 convolution_add_fusion.2
  87.2 1.9 collective-permute-start.6
  89.2 3.9 %collective-permute-start.7 = (bf16[384,256]{1,0:T(8,128)(2,1)S(1)}, bf16[384,256]{1,0:T(8,128)(2,1)S(1)}, u32[]{:S(2)}, u32[]{:S(2)}) collective-permute-start(bf16[384,256]{1,0:T(8,128)(2,1)S(1)} %fusion.13), channel_id=1, source_target_pairs={{32,0},{33,1},{34,2},{35,3},{36,4},{37,5},{38,6},{39,7},{40,8},{41... | collective-permute-start | bytes 589832 | tf_op jit(solution)/shard_map/ppermute | solution.py:20
  94.1 1.3 multiply_convert_fusion.14
  95.7 1.2 fusion.99
  97.3 1.3 multiply_convert_fusion.12
  98.9 1.2 fusion.11
  100.2 0.3 multiply_convert_fusion.10
  100.9 1.0 convolution_convert_fusion.1
  101.9 1.9 collective-permute-start.10
  104.1 1.1 convolution_add_fusion.13
  105.7 1.9 collective-permute-start.9
  107.9 7.5 %collective-permute-start.8 = (bf16[256,256]{1,0:T(8,128)(2,1)S(1)}, bf16[256,256]{1,0:T(8,128)(2,1)S(1)}, u32[]{:S(2)}, u32[]{:S(2)}) collective-permute-start(bf16[256,256]{1,0:T(8,128)(2,1)S(1)} %fusion.19), channel_id=1, source_target_pairs={{0,32},{1,33},{2,34},{3,35},{4,36},{5,37},{6,38},{7,39},{8,40},{9,... | collective-permute-start | bytes 393224 | tf_op jit(solution)/shard_map/ppermute | solution.py:20
  115.8 1.3 multiply_convert_fusion.7
  117.4 1.3 multiply_convert_fusion.5
  119.4 1.3 fusion.10
  121.0 1.4 convolution_add_fusion.22
  122.9 1.0 convolution_convert_fusion
  124.2 2.1 %collective-permute-start.11 = (bf16[384,256]{1,0:T(8,128)(2,1)}, bf16[384,256]{1,0:T(8,128)(2,1)}, u32[]{:S(2)}, u32[]{:S(2)}) collective-permute-start(bf16[384,256]{1,0:T(8,128)(2,1)} %convolution_convert_fusion), channel_id=1, source_target_pairs={{8,0},{9,1},{10,2},{11,3},{12,4},{13,5},{14,6},{15,7},{16,8},{17,9... | collective-permute-start | bytes 589832 | tf_op jit(solution)/shard_map/ppermute | solution.py:20
  126.4 2.1 %fusion.167 = f32[256,512]{0,1:T(8,128)} fusion(bf16[384,256]{1,0:T(8,128)(2,1)} %collective-permute-done, bf16[384,256]{0,1:T(8,128)(2,1)S(1)} %get-tuple-element.40, bf16[384,256]{0,1:T(8,128)(2,1)S(1)} %get-tuple-element.39), kind=kOutput, calls=%fused_computation.258 | convolution fusion | flops 101449728 | bytes 1114112 | tf_op jit(solution)/shard_map/dot_general | solution.py:24
  128.6 1.2 multiply_convert_fusion.22
  130.1 1.2 multiply_convert_fusion.20
  131.5 1.2 fusion.20
  132.7 1.0 multiply_convert_fusion.18
  133.7 1.2 fusion.16
  135.7 0.3 fusion.6
  136.4 0.5 convert_element_type.165
  136.8 1.2 fusion.17
  138.0 0.9 copy.136
  138.9 1.2 fusion.166
  140.0 1.1 fusion.7
  141.1 1.3 copy.117
  142.4 0.9 copy.135
  143.4 1.4 fusion.3
  145.1 0.7 copy-done.6
  145.8 1.1 fusion
  146.9 0.5 convert_element_type.160
  147.3 1.3 pad_maximum_fusion
  148.6 11.2 %all-to-all-start = ((bf16[16,32,1280]{2,1,0:T(8,128)(2,1)}), bf16[16,32,1280]{2,1,0:T(8,128)(2,1)S(1)}, u32[]{:S(2)}, u32[]{:S(2)}) async-start(bf16[16,32,1280]{2,1,0:T(8,128)(2,1)} %pad_maximum_fusion), calls=%async_computation | async-start | bytes 2621440 | tf_op jit(solution)/shard_map/all_to_all | solution.py:144
  160.2 0.6 copy-done.13
  161.6 1.9 collective-permute-start.12
  163.5 1.1 add_convert_fusion
  164.7 10.2 %all-to-all-done = bf16[16,32,1280]{2,1,0:T(8,128)(2,1)S(1)} async-done(((bf16[16,32,1280]{2,1,0:T(8,128)(2,1)}), bf16[16,32,1280]{2,1,0:T(8,128)(2,1)S(1)}, u32[]{:S(2)}, u32[]{:S(2)}) %all-to-all-start) | async-done | bytes 1310752 | tf_op jit(solution)/shard_map/all_to_all | solution.py:144
  175.0 0.5 broadcast.97
  175.5 0.7 reduce.2
  176.2 0.6 reshape.59
  176.8 6.8 %all-to-all-start.1 = ((bf16[32,2,640]{2,1,0:T(2,128)(2,1)}), bf16[32,2,640]{2,1,0:T(2,128)(2,1)S(1)}, u32[]{:S(2)}, u32[]{:S(2)}) async-start(bf16[32,2,640]{2,1,0:T(2,128)(2,1)} %reshape.59), calls=%async_computation.1 | async-start | bytes 163840 | tf_op jit(solution)/shard_map/all_to_all | solution.py:146
  183.9 0.8 maximum_bitcast_fusion
  184.8 14.0 %all-to-all-done.1 = bf16[32,2,640]{2,1,0:T(2,128)(2,1)S(1)} async-done(((bf16[32,2,640]{2,1,0:T(2,128)(2,1)}), bf16[32,2,640]{2,1,0:T(2,128)(2,1)S(1)}, u32[]{:S(2)}, u32[]{:S(2)}) %all-to-all-start.1) | async-done | bytes 81952 | tf_op jit(solution)/shard_map/all_to_all | solution.py:146
  199.0 0.6 fusion.172
  (107 shorter events, 12.0 us)
Async XLA Ops:
  0.6 93.5 %copy-start = (bf16[256,256]{1,0:T(8,128)(2,1)S(1)}, bf16[256,256]{1,0:T(8,128)(2,1)}, u32[]{:S(2)}) copy-start(bf16[256,256]{1,0:T(8,128)(2,1)} %param.11) | copy-start | bytes 393220
  0.6 12.1 %copy-start.2 = (bf16[1,1024,256]{2,1,0:T(8,128)(2,1)S(1)}, bf16[1,1024,256]{2,1,0:T(8,128)(2,1)}, u32[]{:S(2)}) copy-start(bf16[1,1024,256]{2,1,0:T(8,128)(2,1)} %param.6) | copy-start | bytes 1572868
  0.7 12.1 %copy-start.3 = (bf16[2,256,512]{2,1,0:T(8,128)(2,1)S(1)}, bf16[2,256,512]{2,1,0:T(8,128)(2,1)}, u32[]{:S(2)}) copy-start(bf16[2,256,512]{2,1,0:T(8,128)(2,1)} %param.8) | copy-start | bytes 1572868
  3.6 100.4 %collective-permute-start.5 = (bf16[256,256]{1,0:T(8,128)(2,1)}, bf16[256,256]{1,0:T(8,128)(2,1)}, u32[]{:S(2)}, u32[]{:S(2)}) collective-permute-start(bf16[256,256]{1,0:T(8,128)(2,1)} %slice_bitcast_fusion.2), channel_id=1, source_target_pairs={{0,8},{1,9},{2,10},{3,11},{4,12},{5,13},{6,14},{7,15},{8,16},{9,17... | collective-permute-start | bytes 393224 | tf_op jit(solution)/shard_map/ppermute | solution.py:20
  13.8 62.4 %collective-permute-start = (bf16[384,256]{1,0:T(8,128)(2,1)}, bf16[384,256]{1,0:T(8,128)(2,1)}, u32[]{:S(2)}, u32[]{:S(2)}) collective-permute-start(bf16[384,256]{1,0:T(8,128)(2,1)} %get-tuple-element.18), channel_id=1, source_target_pairs={{0,8},{1,9},{2,10},{3,11},{4,12},{5,13},{6,14},{7,15},{8,16},{9,17... | collective-permute-start | bytes 589832 | tf_op jit(solution)/shard_map/ppermute | solution.py:20
  22.9 40.7 %collective-permute-start.1 = (bf16[384,256]{1,0:T(8,128)(2,1)}, bf16[384,256]{1,0:T(8,128)(2,1)}, u32[]{:S(2)}, u32[]{:S(2)}) collective-permute-start(bf16[384,256]{1,0:T(8,128)(2,1)} %get-tuple-element.51), channel_id=1, source_target_pairs={{0,8},{1,9},{2,10},{3,11},{4,12},{5,13},{6,14},{7,15},{8,16},{9,17... | collective-permute-start | bytes 589832 | tf_op jit(solution)/shard_map/ppermute | solution.py:20
  28.2 69.1 %collective-permute-start.4 = (bf16[1024,256]{1,0:T(8,128)(2,1)}, bf16[1024,256]{1,0:T(8,128)(2,1)}, u32[]{:S(2)}, u32[]{:S(2)}) collective-permute-start(bf16[1024,256]{1,0:T(8,128)(2,1)} %bitcast.8), channel_id=1, source_target_pairs={{32,0},{33,1},{34,2},{35,3},{36,4},{37,5},{38,6},{39,7},{40,8},{41... | collective-permute-start | bytes 1572872 | tf_op jit(solution)/shard_map/ppermute | solution.py:20
  31.5 33.6 %copy-start.7 = (bf16[256,256]{1,0:T(8,128)(2,1)S(1)}, bf16[256,256]{1,0:T(8,128)(2,1)}, u32[]{:S(2)}) copy-start(bf16[256,256]{1,0:T(8,128)(2,1)} %param.9) | copy-start | bytes 393220
  64.9 10.7 %copy-start.1 = (bf16[2,256,512]{2,1,0:T(8,128)(2,1)S(1)}, bf16[2,256,512]{2,1,0:T(8,128)(2,1)}, u32[]{:S(2)}) copy-start(bf16[2,256,512]{2,1,0:T(8,128)(2,1)} %param.10) | copy-start | bytes 1572868
  65.4 12.4 %collective-permute-start.2 = (bf16[384,256]{1,0:T(8,128)(2,1)S(1)}, bf16[384,256]{1,0:T(8,128)(2,1)S(1)}, u32[]{:S(2)}, u32[]{:S(2)}) collective-permute-start(bf16[384,256]{1,0:T(8,128)(2,1)S(1)} %fusion.12), channel_id=1, source_target_pairs={{0,32},{1,33},{2,34},{3,35},{4,36},{5,37},{6,38},{7,39},{8,40},{9,... | collective-permute-start | bytes 589832 | tf_op jit(solution)/shard_map/ppermute | solution.py:20
  73.6 11.9 %collective-permute-start.3 = (bf16[384,256]{1,0:T(8,128)(2,1)S(1)}, bf16[384,256]{1,0:T(8,128)(2,1)S(1)}, u32[]{:S(2)}, u32[]{:S(2)}) collective-permute-start(bf16[384,256]{1,0:T(8,128)(2,1)S(1)} %fusion.12), channel_id=1, source_target_pairs={{32,0},{33,1},{34,2},{35,3},{36,4},{37,5},{38,6},{39,7},{40,8},{41... | collective-permute-start | bytes 589832 | tf_op jit(solution)/shard_map/ppermute | solution.py:20
  87.2 16.8 %collective-permute-start.6 = (bf16[384,256]{1,0:T(8,128)(2,1)S(1)}, bf16[384,256]{1,0:T(8,128)(2,1)S(1)}, u32[]{:S(2)}, u32[]{:S(2)}) collective-permute-start(bf16[384,256]{1,0:T(8,128)(2,1)S(1)} %fusion.13), channel_id=1, source_target_pairs={{0,32},{1,33},{2,34},{3,35},{4,36},{5,37},{6,38},{7,39},{8,40},{9,... | collective-permute-start | bytes 589832 | tf_op jit(solution)/shard_map/ppermute | solution.py:20
  89.2 14.9 %collective-permute-start.7 = (bf16[384,256]{1,0:T(8,128)(2,1)S(1)}, bf16[384,256]{1,0:T(8,128)(2,1)S(1)}, u32[]{:S(2)}, u32[]{:S(2)}) collective-permute-start(bf16[384,256]{1,0:T(8,128)(2,1)S(1)} %fusion.13), channel_id=1, source_target_pairs={{32,0},{33,1},{34,2},{35,3},{36,4},{37,5},{38,6},{39,7},{40,8},{41... | collective-permute-start | bytes 589832 | tf_op jit(solution)/shard_map/ppermute | solution.py:20
  100.2 3.6 %copy-start.22 = (bf16[384,256]{1,0:T(8,128)(2,1)}, bf16[384,256]{1,0:T(8,128)(2,1)S(1)}, u32[]{:S(2)}) copy-start(bf16[384,256]{1,0:T(8,128)(2,1)S(1)} %fusion.11) | copy-start | bytes 589828
  100.5 15.2 %copy-start.8 = (bf16[384,256]{0,1:T(8,128)(2,1)}, bf16[384,256]{0,1:T(8,128)(2,1)S(1)}, u32[]{:S(2)}) copy-start(bf16[384,256]{0,1:T(8,128)(2,1)S(1)} %get-tuple-element.33) | copy-start | bytes 589828
  100.5 15.2 %copy-start.10 = (bf16[384,256]{0,1:T(8,128)(2,1)}, bf16[384,256]{0,1:T(8,128)(2,1)S(1)}, u32[]{:S(2)}) copy-start(bf16[384,256]{0,1:T(8,128)(2,1)S(1)} %get-tuple-element.34) | copy-start | bytes 589828
  100.6 3.5 %copy-start.4 = (f32[256,512]{1,0:T(8,128)S(1)}, f32[256,512]{1,0:T(8,128)}, u32[]{:S(2)}) copy-start(f32[256,512]{1,0:T(8,128)} %fusion.93) | copy-start | bytes 1572868
  101.9 46.8 %collective-permute-start.10 = (bf16[384,256]{1,0:T(8,128)(2,1)}, bf16[384,256]{1,0:T(8,128)(2,1)}, u32[]{:S(2)}, u32[]{:S(2)}) collective-permute-start(bf16[384,256]{1,0:T(8,128)(2,1)} %convolution_convert_fusion.1), channel_id=1, source_target_pairs={{8,0},{9,1},{10,2},{11,3},{12,4},{13,5},{14,6},{15,7},{16,8},{17,9... | collective-permute-start | bytes 589832 | tf_op jit(solution)/shard_map/ppermute | solution.py:20
  105.7 24.1 %collective-permute-start.9 = (bf16[256,256]{1,0:T(8,128)(2,1)S(1)}, bf16[256,256]{1,0:T(8,128)(2,1)S(1)}, u32[]{:S(2)}, u32[]{:S(2)}) collective-permute-start(bf16[256,256]{1,0:T(8,128)(2,1)S(1)} %fusion.19), channel_id=1, source_target_pairs={{32,0},{33,1},{34,2},{35,3},{36,4},{37,5},{38,6},{39,7},{40,8},{41... | collective-permute-start | bytes 393224 | tf_op jit(solution)/shard_map/ppermute | solution.py:20
  107.9 20.5 %collective-permute-start.8 = (bf16[256,256]{1,0:T(8,128)(2,1)S(1)}, bf16[256,256]{1,0:T(8,128)(2,1)S(1)}, u32[]{:S(2)}, u32[]{:S(2)}) collective-permute-start(bf16[256,256]{1,0:T(8,128)(2,1)S(1)} %fusion.19), channel_id=1, source_target_pairs={{0,32},{1,33},{2,34},{3,35},{4,36},{5,37},{6,38},{7,39},{8,40},{9,... | collective-permute-start | bytes 393224 | tf_op jit(solution)/shard_map/ppermute | solution.py:20
  120.6 2.1 %copy-start.20 = (bf16[384,256]{1,0:T(8,128)(2,1)}, bf16[384,256]{1,0:T(8,128)(2,1)S(1)}, u32[]{:S(2)}) copy-start(bf16[384,256]{1,0:T(8,128)(2,1)S(1)} %fusion.10) | copy-start | bytes 589828
  121.0 5.4 %copy-start.12 = (bf16[384,256]{0,1:T(8,128)(2,1)}, bf16[384,256]{0,1:T(8,128)(2,1)S(1)}, u32[]{:S(2)}) copy-start(bf16[384,256]{0,1:T(8,128)(2,1)S(1)} %get-tuple-element.39) | copy-start | bytes 589828
  121.0 5.4 %copy-start.14 = (bf16[384,256]{0,1:T(8,128)(2,1)}, bf16[384,256]{0,1:T(8,128)(2,1)S(1)}, u32[]{:S(2)}) copy-start(bf16[384,256]{0,1:T(8,128)(2,1)S(1)} %get-tuple-element.40) | copy-start | bytes 589828
  124.2 24.4 %collective-permute-start.11 = (bf16[384,256]{1,0:T(8,128)(2,1)}, bf16[384,256]{1,0:T(8,128)(2,1)}, u32[]{:S(2)}, u32[]{:S(2)}) collective-permute-start(bf16[384,256]{1,0:T(8,128)(2,1)} %convolution_convert_fusion), channel_id=1, source_target_pairs={{8,0},{9,1},{10,2},{11,3},{12,4},{13,5},{14,6},{15,7},{16,8},{17,9... | collective-permute-start | bytes 589832 | tf_op jit(solution)/shard_map/ppermute | solution.py:20
  132.7 2.2 %copy-start.24 = (bf16[256,256]{1,0:T(8,128)(2,1)}, bf16[256,256]{1,0:T(8,128)(2,1)S(1)}, u32[]{:S(2)}) copy-start(bf16[256,256]{1,0:T(8,128)(2,1)S(1)} %fusion.20) | copy-start | bytes 393220
  136.3 2.5 %copy-start.16 = (bf16[256,256]{1,0:T(8,128)(2,1)S(1)}, bf16[256,256]{1,0:T(8,128)(2,1)}, u32[]{:S(2)}) copy-start(bf16[256,256]{1,0:T(8,128)(2,1)} %get-tuple-element.45) | copy-start | bytes 393220
  136.8 2.0 %copy-start.18 = (bf16[256,256]{1,0:T(8,128)(2,1)S(1)}, bf16[256,256]{1,0:T(8,128)(2,1)}, u32[]{:S(2)}) copy-start(bf16[256,256]{1,0:T(8,128)(2,1)} %get-tuple-element.46) | copy-start | bytes 393220
  141.1 2.2 %copy-start.5 = (f32[256,512]{0,1:T(8,128)S(1)}, f32[256,512]{0,1:T(8,128)}, u32[]{:S(2)}) copy-start(f32[256,512]{0,1:T(8,128)} %fusion.167) | copy-start | bytes 1572868
  144.8 1.0 copy-start.6
  148.6 11.2 %copy-start.9 = (bf16[384,256]{0,1:T(8,128)(2,1)S(1)}, bf16[384,256]{0,1:T(8,128)(2,1)}, u32[]{:S(2)}) copy-start(bf16[384,256]{0,1:T(8,128)(2,1)} %copy-done.8) | copy-start | bytes 589828
  148.6 11.2 %copy-start.11 = (bf16[384,256]{0,1:T(8,128)(2,1)S(1)}, bf16[384,256]{0,1:T(8,128)(2,1)}, u32[]{:S(2)}) copy-start(bf16[384,256]{0,1:T(8,128)(2,1)} %copy-done.10) | copy-start | bytes 589828
  148.6 11.2 %copy-start.23 = (bf16[384,256]{1,0:T(8,128)(2,1)S(1)}, bf16[384,256]{1,0:T(8,128)(2,1)}, u32[]{:S(2)}) copy-start(bf16[384,256]{1,0:T(8,128)(2,1)} %copy-done.22) | copy-start | bytes 589828
  148.6 26.2 %all-to-all-start = ((bf16[16,32,1280]{2,1,0:T(8,128)(2,1)}), bf16[16,32,1280]{2,1,0:T(8,128)(2,1)S(1)}, u32[]{:S(2)}, u32[]{:S(2)}) async-start(bf16[16,32,1280]{2,1,0:T(8,128)(2,1)} %pad_maximum_fusion), calls=%async_computation | async-start | bytes 2621440 | tf_op jit(solution)/shard_map/all_to_all | solution.py:144
  159.9 0.9 copy-start.13
  159.9 1.0 copy-start.15
  159.9 1.1 copy-start.21
  159.9 1.4 copy-start.17
  159.9 1.4 copy-start.19
  161.6 22.0 %collective-permute-start.12 = (bf16[256,256]{1,0:T(8,128)(2,1)S(1)}, bf16[256,256]{1,0:T(8,128)(2,1)S(1)}, u32[]{:S(2)}, u32[]{:S(2)}) collective-permute-start(bf16[256,256]{1,0:T(8,128)(2,1)S(1)} %convolution_convert_fusion.4), channel_id=1, source_target_pairs={{8,0},{9,1},{10,2},{11,3},{12,4},{13,5},{14,6},{15,7},{16,8},{17,9... | collective-permute-start | bytes 393224 | tf_op jit(solution)/shard_map/ppermute | solution.py:20
  164.6 19.0 %copy-start.25 = (bf16[256,256]{1,0:T(8,128)(2,1)S(1)}, bf16[256,256]{1,0:T(8,128)(2,1)}, u32[]{:S(2)}) copy-start(bf16[256,256]{1,0:T(8,128)(2,1)} %copy-done.24) | copy-start | bytes 393220
  176.8 21.9 %all-to-all-start.1 = ((bf16[32,2,640]{2,1,0:T(2,128)(2,1)}), bf16[32,2,640]{2,1,0:T(2,128)(2,1)S(1)}, u32[]{:S(2)}, u32[]{:S(2)}) async-start(bf16[32,2,640]{2,1,0:T(2,128)(2,1)} %reshape.59), calls=%async_computation.1 | async-start | bytes 163840 | tf_op jit(solution)/shard_map/all_to_all | solution.py:146

commit v3 on v1

v3 whole, which is shorter than its diff:
```python
import functools

import jax
import jax.numpy as jnp
from jax import lax
from jax.experimental import pallas as pl
from jax.experimental.pallas import tpu as pltpu
from jax.sharding import Mesh
from jax.sharding import PartitionSpec as P

SHIFT = 3
TILE = 512
BESIDE = 2 * 10**10
VMEM_LIMIT = 16 * 1024 * 1024
LANES = 128


def split_axes(mesh):
    blocks = mesh.devices.shape[1]
    member = min(32, blocks // 2)
    split = mesh.devices.reshape(mesh.devices.shape[0], blocks // member, member)
    return Mesh(split, ("dp", "group", "member"))


def move(block, route):
    return lax.ppermute(block, ("group", "member"), route)


def contract_rows(left, right):
    return lax.dot_general(
        left, right, (((0,), (0,)), ((), ())), preferred_element_type=jnp.float32
    )


def contract_cols(left, right):
    return lax.dot_general(
        left, right, (((1,), (1,)), ((), ())), preferred_element_type=jnp.float32
    )


def gates(current, earlier, conv_weight):
    pre = jnp.dot(earlier, conv_weight[0], preferred_element_type=jnp.float32) + jnp.dot(
        current, conv_weight[1], preferred_element_type=jnp.float32
    )
    return halves(pre)


def halves(pre):
    half_width = pre.shape[1] // 2
    return jnp.tanh(pre[:, :half_width]), jax.nn.sigmoid(pre[:, half_width:])


def gate_gradient(tanh_part, sig_part, grad_gated):
    return jnp.concatenate(
        [
            grad_gated * sig_part * (1.0 - tanh_part * tanh_part),
            grad_gated * tanh_part * sig_part * (1.0 - sig_part),
        ],
        axis=1,
    ).astype(jnp.bfloat16)


def tiles(rows):
    step = min(TILE, rows)
    return [pl.ds(start, step) for start in range(0, rows, step)]


def prepare_kernel(x_ref, conv_ref, own_ref):
    for part in tiles(x_ref.shape[0]):
        own_ref[part] = jnp.dot(x_ref[part], conv_ref[1], preferred_element_type=jnp.float32)


def ahead_kernel(cot_ref, proj_ref, gated_ref):
    for part in tiles(cot_ref.shape[0]):
        gated_ref[part] = contract_cols(cot_ref[part], proj_ref[...])


def forward_kernel(
    x_ref, past_ref, own_ref, conv_ref, proj_ref, middle_ref, gated_ref, tanh_ref, sig_ref
):
    for part in tiles(x_ref.shape[0]):
        t, s = halves(
            jnp.dot(past_ref[part], conv_ref[0], preferred_element_type=jnp.float32)
            + own_ref[part]
        )
        tanh_ref[part] = t
        sig_ref[part] = s
        gated = (t * s).astype(jnp.bfloat16)
        gated_ref[part] = gated
        middle_ref[part] = (
            x_ref[part].astype(jnp.float32)
            + jnp.dot(gated, proj_ref[...], preferred_element_type=jnp.float32)
        ).astype(jnp.bfloat16)


def backward_kernel(
    middle_ref,
    middle_past_ref,
    middle_ahead_ref,
    cot_ref,
    gated_ahead_ref,
    tanh_ref,
    sig_ref,
    conv_first_ref,
    proj_first_ref,
    conv_second_ref,
    proj_second_ref,
    tap_ref,
    direct_ref,
    gated_second_ref,
    pre_second_ref,
    grad_ref,
    pre_first_ref,
):
    for part in tiles(middle_ref.shape[0]):
        middle, cot = middle_ref[part], cot_ref[part]
        t, s = gates(middle_ahead_ref[part], middle, conv_second_ref)
        ahead = gate_gradient(t, s, gated_ahead_ref[part])
        back = contract_cols(ahead, conv_second_ref[0]).astype(jnp.bfloat16)
        t, s = gates(middle, middle_past_ref[part], conv_second_ref)
        gated_second_ref[part] = (t * s).astype(jnp.bfloat16)
        here = gate_gradient(t, s, contract_cols(cot, proj_second_ref[...]))
        pre_second_ref[part] = here
        grad = (
            cot.astype(jnp.float32)
            + contract_cols(here, conv_second_ref[1])
            + back.astype(jnp.float32)
        ).astype(jnp.bfloat16)
        grad_ref[part] = grad
        here = gate_gradient(
            tanh_ref[part], sig_ref[part], contract_cols(grad, proj_first_ref[...])
        )
        pre_first_ref[part] = here
        tap_ref[part] = contract_cols(here, conv_first_ref[0]).astype(jnp.bfloat16)
        direct_ref[part] = (
            grad.astype(jnp.float32) + contract_cols(here, conv_first_ref[1])
        ).astype(jnp.bfloat16)


def weights_kernel(scale, *refs):
    inputs, (sent_ref, lines, square) = refs[:-3], refs[-3:]

    def total(left, right):
        return contract_rows(left[...], right[...]) * scale

    share = sent_ref.shape[2]
    for layer in range(2):
        past, current, pre, gated, grad = inputs[layer * 5 : layer * 5 + 5]
        inner, width = past.shape[1], pre.shape[1]
        lines[:inner] = total(past, pre)
        lines[inner : 2 * inner] = total(current, pre)
        proj = total(gated, grad)
        columns = proj.shape[1]
        per_line = width // columns
        for i in range(columns // LANES):
            square[...] = proj[:, i * LANES : (i + 1) * LANES]
            for j in range(per_line):
                at = j * columns + i * LANES
                lines[2 * inner :, at : at + LANES] = square[
                    pl.ds(j, inner // per_line, stride=per_line)
                ]
        for part in range(sent_ref.shape[0]):
            sent_ref[part, layer] = lines[part * share : (part + 1) * share].astype(jnp.bfloat16)


def stage_kernel(received_ref, _, sent_ref, flat, slots):
    devices, layers, rows, width = received_ref.shape
    members, slot, _ = sent_ref.shape
    across = width // LANES
    share = rows * across // members
    slots[...] = jnp.zeros_like(slots)
    for layer in range(layers):
        total = jnp.sum(received_ref[:, layer].astype(jnp.float32), axis=0)
        for i in range(across):
            flat[pl.ds(i, rows, stride=across)] = total[:, i * LANES : (i + 1) * LANES]
        for j in range(share):
            slots[pl.ds(layer * share + j, members, stride=slot)] = flat[
                pl.ds(j, members, stride=share)
            ]
    for i in range(members):
        sent_ref[i] = slots[i * slot : (i + 1) * slot].astype(jnp.bfloat16)


def finish_kernel(received_ref, sums_ref):
    sums_ref[...] = jnp.sum(received_ref[...].astype(jnp.float32), axis=0)


def copy_kernel(from_ref, to_ref):
    to_ref[...] = from_ref[...]


def add_kernel(direct_ref, back_ref, grad_ref):
    grad_ref[...] = (
        direct_ref[...].astype(jnp.float32) + back_ref[...].astype(jnp.float32)
    ).astype(jnp.bfloat16)


def call(kernel, outs, *args, scratch=(), flops=0, after=0):
    moved = sum(a.size * a.dtype.itemsize for a in (*args, *outs))
    here = pl.BlockSpec(memory_space=pltpu.VMEM)
    waited = [pl.BlockSpec(memory_space=pl.ANY)] * after
    return pl.pallas_call(
        kernel,
        out_shape=tuple(outs),
        in_specs=[here] * (len(args) - after) + waited,
        out_specs=(here,) * len(outs),
        scratch_shapes=list(scratch),
        compiler_params=pltpu.CompilerParams(vmem_limit_bytes=VMEM_LIMIT),
        cost_estimate=pl.CostEstimate(flops=flops, bytes_accessed=moved, transcendentals=0),
    )(*args)


def per_device(x, cotangent, conv_first, proj_first, conv_second, proj_second):
    shape = x.shape
    channels, width = shape[2], conv_first.shape[2]
    rows = shape[0] * shape[1]
    parts = lax.axis_size("dp") * lax.axis_size("group")
    members = lax.axis_size("member")
    blocks = lax.axis_size("group") * members
    near = min(8, blocks // 16)
    far = min(32, blocks // 4)
    scale = float(rows * lax.axis_size("dp") * blocks) ** (-0.5)
    array, bf16, f32 = jax.ShapeDtypeStruct, jnp.bfloat16, jnp.float32

    def place(block):
        group, member = divmod(block, members)
        return group * members + (member - SHIFT) % members

    def pairs(span):
        return [(i, i + span) for i in range(blocks) if i + span in range(blocks)]

    narrow, wide = array((rows, channels), bf16), array((rows, width), bf16)
    single, double = array((rows, channels), f32), array((rows, width), f32)
    x, cot = x.reshape(rows, channels), cotangent.reshape(rows, channels)
    homes = [(i, place(i)) for i in range(blocks)]
    past = move(x, [(i, place(j)) for i, j in pairs(near)])
    x = move(x, homes)
    cot = move(cot, homes)
    cot_ahead = move(cot, [(place(i), place(j)) for i, j in pairs(-far)])
    (own,) = call(
        prepare_kernel, (double,), x, conv_first, flops=4 * rows * channels * channels
    )
    (gated_ahead,) = call(ahead_kernel, (single,), cot_ahead, proj_second, flops=BESIDE)
    middle, gated, tanh_part, sig_part = call(
        forward_kernel,
        (narrow, narrow, single, single),
        x,
        past,
        own,
        conv_first,
        proj_first,
        flops=6 * rows * channels * channels,
    )
    middle_past = move(middle, [(place(i), place(j)) for i, j in pairs(far)])
    middle_ahead = move(middle, [(place(i), place(j)) for i, j in pairs(-far)])
    tap, direct, gated_second, pre_second, grad, pre_first = call(
        backward_kernel,
        (narrow, narrow, narrow, wide, narrow, wide),
        middle,
        middle_past,
        middle_ahead,
        cot,
        gated_ahead,
        tanh_part,
        sig_part,
        conv_first,
        proj_first,
        conv_second,
        proj_second,
        flops=38 * rows * channels * channels,
    )
    tap_back = move(tap, [(place(j), i) for i, j in pairs(near)])
    direct = move(direct, [(j, i) for i, j in homes])
    weight_rows = 2 * channels + channels * channels // width
    (sent,) = call(
        functools.partial(weights_kernel, scale),
        (array((parts, 2, weight_rows // parts, width), bf16),),
        past,
        x,
        pre_first,
        gated,
        grad,
        middle_past,
        middle,
        pre_second,
        gated_second,
        cot,
        scratch=[pltpu.VMEM((weight_rows, width), f32), pltpu.VMEM((channels, LANES), f32)],
        flops=rows * channels * 20 * channels,
    )
    received = lax.all_to_all(sent, ("dp", "group"), 0, 0, tiled=True)
    share = weight_rows * width // (parts * members * LANES)
    slot = -(-2 * share // 16) * 16
    (tap_back,) = call(copy_kernel, (narrow,), tap_back, flops=BESIDE)
    (grad_x,) = call(add_kernel, (narrow,), direct, tap_back, flops=BESIDE)
    (sent,) = call(
        stage_kernel,
        (array((members, slot, LANES), bf16),),
        received,
        tap_back,
        scratch=[
            pltpu.VMEM((members * share, LANES), f32),
            pltpu.VMEM((members * slot, LANES), f32),
        ],
        after=1,
    )
    received = lax.all_to_all(sent, "member", 0, 0, tiled=True)
    (sums,) = call(finish_kernel, (array((slot, LANES), f32),), received)
    return (
        grad_x.reshape(shape),
        sums[:share].reshape(-1),
        sums[share : 2 * share].reshape(-1),
    )


def solution(mesh):
    time, flat = P("dp", ("group", "member"), None), P(("dp", "group", "member"))
    return jax.shard_map(
        per_device,
        mesh=split_axes(mesh),
        in_specs=(time, time, P(), P(), P(), P()),
        out_specs=(time, flat, flat),
        check_vma=False,
    )
```

time: 164 us -> 141 us (0.86)
  starting transfers between devices: 81.2 us -> 56 us
  waiting for transfers between devices: 57.3 us -> 72.5 us
  matrix products: 14.7 us -> 0 us
  Pallas kernels: 0 us -> 9.44 us
  local copies, waits for them, and re-layouts: 7.12 us -> 1.67 us
  other arithmetic: 1.66 us -> 0 us
    ppermute x5 -> x8, starting transfers between devices: 54.5 us -> 36.3 us  [move(): return lax.ppermute(block, ('group', 'member'), route)]
    dot_general x20 -> x0, matrix products: 14.7 us -> none  [the longest x7 6.87 us: contract_cols(): lax.dot_general(left, right, (((1,), (1,)), ((), ())), preferred_element_...]
    ppermute x5 -> x8, waiting for transfers between devices: 37.7 us -> 51.6 us  [move(): return lax.ppermute(block, ('group', 'member'), route)]
    pallas_call x0 -> x9, Pallas kernels: none -> 9.44 us  [call(): pl.pallas_call(kernel, out_shape=tuple(outs), in_specs=[here] * (len(args...]
    all_to_all x2 -> x1, starting transfers between devices: 14.3 us -> 7.95 us  [per_device(): received = lax.all_to_all(sent, ('dp', 'group'), 0, 0, tiled=True)]
    all_to_all x1, waiting for transfers between devices: 12.7 us -> 16.3 us  [per_device(): received = lax.all_to_all(sent, 'member', 0, 0, tiled=True)]
    convert_element_type x2 -> x0, local copies, waits for them, and re-layouts: 2.64 us -> none  [sum_first_stage(): (terms * scale).astype(jnp.bfloat16)]
    all_to_all x2 -> x1, waiting for transfers between devices: 6.84 us -> 4.52 us  [per_device(): received = lax.all_to_all(sent, ('dp', 'group'), 0, 0, tiled=True)]
  transfers between devices with their start and end apart: 8 -> 10, of which waited for: 6 -> 8; matrix products, arithmetic and copies ran while one was open for 8% -> 0% of each run, Pallas kernels for 0% -> 4%
where the time goes in v3:
time: 141 us; the launch traced here: 140 us
  waiting for transfers between devices  72.5 us (51%)
  starting transfers between devices  56 us (40%)
  Pallas kernels  9.44 us (7%)
  local copies, waits for them, and re-layouts  1.67 us (1%)
    ppermute x8, waiting for transfers between devices, move(): return lax.ppermute(block, ('group', 'member'), route)  51.6 us
    ppermute x8, starting transfers between devices, move(): return lax.ppermute(block, ('group', 'member'), route)  36.3 us
    all_to_all x1, waiting for transfers between devices, per_device(): received = lax.all_to_all(sent, 'member', 0, 0, tiled=True)  16.3 us
    all_to_all x1, starting transfers between devices, per_device(): received = lax.all_to_all(sent, 'member', 0, 0, tiled=True)  11.8 us
    pallas_call x9, Pallas kernels, call(): pl.pallas_call(kernel, out_shape=tuple(outs), in_specs=[here] * (len(args...  9.44 us
    all_to_all x1, starting transfers between devices, per_device(): received = lax.all_to_all(sent, ('dp', 'group'), 0, 0, tiled=True)  7.95 us
    all_to_all x1, waiting for transfers between devices, per_device(): received = lax.all_to_all(sent, ('dp', 'group'), 0, 0, tiled=True)  4.52 us
  transfers between devices with their start and end apart: 10, of which 8 were waited for; matrix products, arithmetic and copies ran while one was open for 0% of the time, Pallas kernels for 4%

profile of v3, /device:TPU:6, one launch (start us, length us, event | category | flops | bytes accessed | tf_op | source)
XLA Modules:
  0.0 140.4 jit_solution(565976521483944072)
XLA Ops:
  0.6 11.3 %collective-permute-start.4 = (bf16[1024,256]{1,0:T(8,128)(2,1)}, bf16[1024,256]{1,0:T(8,128)(2,1)S(1)}, u32[]{:S(2)}, u32[]{:S(2)}) collective-permute-start(bf16[1024,256]{1,0:T(8,128)(2,1)} %bitcast.7), channel_id=1, source_target_pairs={{0,29},{1,30},{2,31},{3,0},{4,1},{5,2},{6,3},{7,4},{8,5},{9,6},{10... | collective-permute-start | bytes 1572872 | tf_op jit(solution)/shard_map/ppermute | solution.py:26
  11.9 3.2 %collective-permute-start = (bf16[1024,256]{1,0:T(8,128)(2,1)}, bf16[1024,256]{1,0:T(8,128)(2,1)S(1)}, u32[]{:S(2)}, u32[]{:S(2)}) collective-permute-start(bf16[1024,256]{1,0:T(8,128)(2,1)} %bitcast.8), channel_id=1, source_target_pairs={{0,29},{1,30},{2,31},{3,0},{4,1},{5,2},{6,3},{7,4},{8,5},{9,6},{10... | collective-permute-start | bytes 1572872 | tf_op jit(solution)/shard_map/ppermute | solution.py:26
  15.1 2.8 %collective-permute-start.1 = (bf16[1024,256]{1,0:T(8,128)(2,1)}, bf16[1024,256]{1,0:T(8,128)(2,1)S(1)}, u32[]{:S(2)}, u32[]{:S(2)}) collective-permute-start(bf16[1024,256]{1,0:T(8,128)(2,1)} %bitcast.9), channel_id=1, source_target_pairs={{0,5},{1,6},{2,7},{3,8},{4,9},{5,10},{6,11},{7,12},{8,13},{9,14},{... | collective-permute-start | bytes 1572872 | tf_op jit(solution)/shard_map/ppermute | solution.py:26
  18.0 12.8 %collective-permute-done.4.cot_ref.refs_9_ = bf16[1024,256]{1,0:T(8,128)(2,1)S(1)} collective-permute-done((bf16[1024,256]{1,0:T(8,128)(2,1)}, bf16[1024,256]{1,0:T(8,128)(2,1)S(1)}, u32[]{:S(2)}, u32[]{:S(2)}) %collective-permute-start.4) | collective-permute-done | bytes 524320 | tf_op jit(solution)/shard_map/ppermute | solution.py:26
  30.7 2.7 %collective-permute-start.5 = (bf16[1024,256]{1,0:T(8,128)(2,1)S(1)}, bf16[1024,256]{1,0:T(8,128)(2,1)S(1)}, u32[]{:S(2)}, u32[]{:S(2)}) collective-permute-start(bf16[1024,256]{1,0:T(8,128)(2,1)S(1)} %collective-permute-done.4.cot_ref.refs_9_), channel_id=1, source_target_pairs={{61,29},{62,30},{63,31},{32,0},{33,1},{34,2},{35,3},{36,4},{37,5},... | collective-permute-start | bytes 1572872 | tf_op jit(solution)/shard_map/ppermute | solution.py:26
  33.4 13.1 %collective-permute-done.x_ref.refs_1_ = bf16[1024,256]{1,0:T(8,128)(2,1)S(1)} collective-permute-done((bf16[1024,256]{1,0:T(8,128)(2,1)}, bf16[1024,256]{1,0:T(8,128)(2,1)S(1)}, u32[]{:S(2)}, u32[]{:S(2)}) %collective-permute-start) | collective-permute-done | bytes 524320 | tf_op jit(solution)/shard_map/ppermute | solution.py:26
  46.5 0.0 copy-start
  46.5 1.0 copy-done
  47.6 0.0 copy-start.2
  47.6 0.4 shard_map.85.own_ref
  48.0 0.0 copy-start.4
  48.0 2.5 %collective-permute-done.1.past_ref.refs_0_ = bf16[1024,256]{1,0:T(8,128)(2,1)S(1)} collective-permute-done((bf16[1024,256]{1,0:T(8,128)(2,1)}, bf16[1024,256]{1,0:T(8,128)(2,1)S(1)}, u32[]{:S(2)}, u32[]{:S(2)}) %collective-permute-start.1) | collective-permute-done | bytes 524320 | tf_op jit(solution)/shard_map/ppermute | solution.py:26
  50.6 0.0 copy-done.2
  50.6 0.7 shard_map.86
  51.3 0.0 copy-start.1
  51.3 0.0 copy-start.3
  51.3 2.9 %collective-permute-start.3 = (bf16[1024,256]{1,0:T(8,128)(2,1)S(1)}, bf16[1024,256]{1,0:T(8,128)(2,1)S(1)}, u32[]{:S(2)}, u32[]{:S(2)}) collective-permute-start(bf16[1024,256]{1,0:T(8,128)(2,1)S(1)} %get-tuple-element.13.middle_ref.refs_6_), channel_id=1, source_target_pairs={{61,29},{62,30},{63,31},{32,0},{33,1},{34,2},{35,3},{36,4},{37,5},... | collective-permute-start | bytes 1572872 | tf_op jit(solution)/shard_map/ppermute | solution.py:26
  54.2 7.7 %collective-permute-start.2 = (bf16[1024,256]{1,0:T(8,128)(2,1)S(1)}, bf16[1024,256]{1,0:T(8,128)(2,1)S(1)}, u32[]{:S(2)}, u32[]{:S(2)}) collective-permute-start(bf16[1024,256]{1,0:T(8,128)(2,1)S(1)} %get-tuple-element.13.middle_ref.refs_6_), channel_id=1, source_target_pairs={{29,61},{30,62},{31,63},{0,32},{1,33},{2,34},{3,35},{4,36},{5,37},... | collective-permute-start | bytes 1572872 | tf_op jit(solution)/shard_map/ppermute | solution.py:26
  61.9 0.0 collective-permute-done.5.cot_ref
  61.9 0.0 copy-done.4
  61.9 0.3 shard_map.87.gated_ahead_ref
  62.3 9.9 %collective-permute-done.3.middle_ahead_ref = bf16[1024,256]{1,0:T(8,128)(2,1)S(1)} collective-permute-done((bf16[1024,256]{1,0:T(8,128)(2,1)S(1)}, bf16[1024,256]{1,0:T(8,128)(2,1)S(1)}, u32[]{:S(2)}, u32[]{:S(2)}) %collective-permute-start.3) | collective-permute-done | bytes 524320 | tf_op jit(solution)/shard_map/ppermute | solution.py:26
  72.2 1.2 collective-permute-done.2.middle_past_ref.refs_5_
  73.4 0.0 copy-done.1
  73.4 0.0 copy-done.3
  73.4 3.4 %shard_map.88 = (bf16[1024,256]{1,0:T(8,128)(2,1)S(1)}, bf16[1024,256]{1,0:T(8,128)(2,1)S(1)}, bf16[1024,256]{1,0:T(8,128)(2,1)S(1)}, bf16[1024,512]{1,0:T(8,128...) custom-call(bf16[1024,256]{1,0:T(8,128)(2,1)S(1)} %get-tuple-element.13.middle_ref.refs_6_, ...), custom_call_target="tpu_custom_call" | custom-call | flops 2550136832 | bytes 10747904 | tf_op jit(solution)/shard_map/pallas_call | solution.py:202
  76.7 1.9 %collective-permute-start.7 = (bf16[1024,256]{1,0:T(8,128)(2,1)S(1)}, bf16[1024,256]{1,0:T(8,128)(2,1)S(1)}, u32[]{:S(2)}, u32[]{:S(2)}) collective-permute-start(bf16[1024,256]{1,0:T(8,128)(2,1)S(1)} %get-tuple-element.17), channel_id=1, source_target_pairs={{5,0},{6,1},{7,2},{8,3},{9,4},{10,5},{11,6},{12,7},{13,8},{14,9},{... | collective-permute-start | bytes 1572872 | tf_op jit(solution)/shard_map/ppermute | solution.py:26
  78.7 2.7 %shard_map.91 = bf16[16,2,40,512]{3,2,1,0:T(8,128)(2,1)} custom-call(bf16[1024,256]{1,0:T(8,128)(2,1)S(1)} %collective-permute-done.1.past_ref.refs_0_, bf16[1024,256]{1,0:T(8,128)(2,1)S(1)} %collective-permute-done.x_ref.refs_1_, bf16[1024,512]{1,0:T(8,128)(2,1)S(1)} %get-tuple-element.18.refs_2_, bf16[1024,256]{1,0:T(8,128)(2,1)S(1)} %get-tuple-element.19.refs_3_, ...), custom_call_target="tpu_custom_call" | custom-call | flops 1342177280 | bytes 7602176 | tf_op jit(solution)/shard_map/pallas_call | solution.py:202
  81.4 8.0 %all-to-all-start = ((bf16[16,2,40,512]{3,2,1,0:T(8,128)(2,1)}), bf16[16,2,40,512]{3,2,1,0:T(8,128)(2,1)S(1)}, u32[]{:S(2)}, u32[]{:S(2)}) async-start(bf16[16,2,40,512]{3,2,1,0:T(8,128)(2,1)} %shard_map.91), calls=%async_computation | async-start | bytes 2621440 | tf_op jit(solution)/shard_map/all_to_all | solution.py:291
  89.3 3.7 %collective-permute-start.6 = (bf16[1024,256]{1,0:T(8,128)(2,1)S(1)}, bf16[1024,256]{1,0:T(8,128)(2,1)S(1)}, u32[]{:S(2)}, u32[]{:S(2)}) collective-permute-start(bf16[1024,256]{1,0:T(8,128)(2,1)S(1)} %get-tuple-element.16), channel_id=1, source_target_pairs={{29,0},{30,1},{31,2},{0,3},{1,4},{2,5},{3,6},{4,7},{5,8},{6,9},{7,... | collective-permute-start | bytes 1572872 | tf_op jit(solution)/shard_map/ppermute | solution.py:26
  93.1 12.2 %collective-permute-done.7.from_ref = bf16[1024,256]{1,0:T(8,128)(2,1)S(1)} collective-permute-done((bf16[1024,256]{1,0:T(8,128)(2,1)S(1)}, bf16[1024,256]{1,0:T(8,128)(2,1)S(1)}, u32[]{:S(2)}, u32[]{:S(2)}) %collective-permute-start.7) | collective-permute-done | bytes 524320 | tf_op jit(solution)/shard_map/ppermute | solution.py:26
  105.3 4.5 %all-to-all-done.received_ref = bf16[16,2,40,512]{3,2,1,0:T(8,128)(2,1)S(1)} async-done(((bf16[16,2,40,512]{3,2,1,0:T(8,128)(2,1)}), bf16[16,2,40,512]{3,2,1,0:T(8,128)(2,1)S(1)}, u32[]{:S(2)}, u32[]{:S(2)}) %all-to-all-start) | async-done | bytes 1310752 | tf_op jit(solution)/shard_map/all_to_all | solution.py:291
  109.8 0.9 shard_map.92
  110.7 11.8 %all-to-all-start.1 = ((bf16[32,16,128]{2,1,0:T(8,128)(2,1)}), bf16[32,16,128]{2,1,0:T(8,128)(2,1)S(1)}, u32[]{:S(2)}, u32[]{:S(2)}) async-start(bf16[32,16,128]{2,1,0:T(8,128)(2,1)} %shard_map.92), calls=%async_computation.1 | async-start | bytes 262144 | tf_op jit(solution)/shard_map/all_to_all | solution.py:307
  122.5 0.0 collective-permute-done.6.direct_ref
  122.5 0.9 shard_map.90
  123.5 16.3 %all-to-all-done.1.received_ref = bf16[32,16,128]{2,1,0:T(8,128)(2,1)S(1)} async-done(((bf16[32,16,128]{2,1,0:T(8,128)(2,1)}), bf16[32,16,128]{2,1,0:T(8,128)(2,1)S(1)}, u32[]{:S(2)}, u32[]{:S(2)}) %all-to-all-start.1) | async-done | bytes 131104 | tf_op jit(solution)/shard_map/all_to_all | solution.py:307
  139.8 0.6 slice_bitcast_fusion
  (2 shorter events, 0.1 us)
Async XLA Ops:
  0.6 30.1 %collective-permute-start.4 = (bf16[1024,256]{1,0:T(8,128)(2,1)}, bf16[1024,256]{1,0:T(8,128)(2,1)S(1)}, u32[]{:S(2)}, u32[]{:S(2)}) collective-permute-start(bf16[1024,256]{1,0:T(8,128)(2,1)} %bitcast.7), channel_id=1, source_target_pairs={{0,29},{1,30},{2,31},{3,0},{4,1},{5,2},{6,3},{7,4},{8,5},{9,6},{10... | collective-permute-start | bytes 1572872 | tf_op jit(solution)/shard_map/ppermute | solution.py:26
  11.9 34.6 %collective-permute-start = (bf16[1024,256]{1,0:T(8,128)(2,1)}, bf16[1024,256]{1,0:T(8,128)(2,1)S(1)}, u32[]{:S(2)}, u32[]{:S(2)}) collective-permute-start(bf16[1024,256]{1,0:T(8,128)(2,1)} %bitcast.8), channel_id=1, source_target_pairs={{0,29},{1,30},{2,31},{3,0},{4,1},{5,2},{6,3},{7,4},{8,5},{9,6},{10... | collective-permute-start | bytes 1572872 | tf_op jit(solution)/shard_map/ppermute | solution.py:26
  15.1 35.4 %collective-permute-start.1 = (bf16[1024,256]{1,0:T(8,128)(2,1)}, bf16[1024,256]{1,0:T(8,128)(2,1)S(1)}, u32[]{:S(2)}, u32[]{:S(2)}) collective-permute-start(bf16[1024,256]{1,0:T(8,128)(2,1)} %bitcast.9), channel_id=1, source_target_pairs={{0,5},{1,6},{2,7},{3,8},{4,9},{5,10},{6,11},{7,12},{8,13},{9,14},{... | collective-permute-start | bytes 1572872 | tf_op jit(solution)/shard_map/ppermute | solution.py:26
  30.7 31.2 %collective-permute-start.5 = (bf16[1024,256]{1,0:T(8,128)(2,1)S(1)}, bf16[1024,256]{1,0:T(8,128)(2,1)S(1)}, u32[]{:S(2)}, u32[]{:S(2)}) collective-permute-start(bf16[1024,256]{1,0:T(8,128)(2,1)S(1)} %collective-permute-done.4.cot_ref.refs_9_), channel_id=1, source_target_pairs={{61,29},{62,30},{63,31},{32,0},{33,1},{34,2},{35,3},{36,4},{37,5},... | collective-permute-start | bytes 1572872 | tf_op jit(solution)/shard_map/ppermute | solution.py:26
  46.5 1.0 copy-start
  47.6 3.0 %copy-start.2 = (bf16[256,256]{1,0:T(8,128)(2,1)S(1)}, bf16[256,256]{1,0:T(8,128)(2,1)}, u32[]{:S(2)}) copy-start(bf16[256,256]{1,0:T(8,128)(2,1)} %proj_first_ref.1) | copy-start | bytes 393220
  48.0 13.9 %copy-start.4 = (bf16[256,256]{1,0:T(8,128)(2,1)S(1)}, bf16[256,256]{1,0:T(8,128)(2,1)}, u32[]{:S(2)}) copy-start(bf16[256,256]{1,0:T(8,128)(2,1)} %proj_second_ref.1) | copy-start | bytes 393220
  51.3 22.1 %copy-start.1 = (bf16[2,256,512]{2,1,0:T(8,128)(2,1)S(1)}, bf16[2,256,512]{2,1,0:T(8,128)(2,1)}, u32[]{:S(2)}) copy-start(bf16[2,256,512]{2,1,0:T(8,128)(2,1)} %conv_first_ref.1) | copy-start | bytes 1572868
  51.3 22.1 %copy-start.3 = (bf16[2,256,512]{2,1,0:T(8,128)(2,1)S(1)}, bf16[2,256,512]{2,1,0:T(8,128)(2,1)}, u32[]{:S(2)}) copy-start(bf16[2,256,512]{2,1,0:T(8,128)(2,1)} %conv_second_ref.1) | copy-start | bytes 1572868
  51.3 20.9 %collective-permute-start.3 = (bf16[1024,256]{1,0:T(8,128)(2,1)S(1)}, bf16[1024,256]{1,0:T(8,128)(2,1)S(1)}, u32[]{:S(2)}, u32[]{:S(2)}) collective-permute-start(bf16[1024,256]{1,0:T(8,128)(2,1)S(1)} %get-tuple-element.13.middle_ref.refs_6_), channel_id=1, source_target_pairs={{61,29},{62,30},{63,31},{32,0},{33,1},{34,2},{35,3},{36,4},{37,5},... | collective-permute-start | bytes 1572872 | tf_op jit(solution)/shard_map/ppermute | solution.py:26
  54.2 19.2 %collective-permute-start.2 = (bf16[1024,256]{1,0:T(8,128)(2,1)S(1)}, bf16[1024,256]{1,0:T(8,128)(2,1)S(1)}, u32[]{:S(2)}, u32[]{:S(2)}) collective-permute-start(bf16[1024,256]{1,0:T(8,128)(2,1)S(1)} %get-tuple-element.13.middle_ref.refs_6_), channel_id=1, source_target_pairs={{29,61},{30,62},{31,63},{0,32},{1,33},{2,34},{3,35},{4,36},{5,37},... | collective-permute-start | bytes 1572872 | tf_op jit(solution)/shard_map/ppermute | solution.py:26
  76.7 28.5 %collective-permute-start.7 = (bf16[1024,256]{1,0:T(8,128)(2,1)S(1)}, bf16[1024,256]{1,0:T(8,128)(2,1)S(1)}, u32[]{:S(2)}, u32[]{:S(2)}) collective-permute-start(bf16[1024,256]{1,0:T(8,128)(2,1)S(1)} %get-tuple-element.17), channel_id=1, source_target_pairs={{5,0},{6,1},{7,2},{8,3},{9,4},{10,5},{11,6},{12,7},{13,8},{14,9},{... | collective-permute-start | bytes 1572872 | tf_op jit(solution)/shard_map/ppermute | solution.py:26
  81.4 28.4 %all-to-all-start = ((bf16[16,2,40,512]{3,2,1,0:T(8,128)(2,1)}), bf16[16,2,40,512]{3,2,1,0:T(8,128)(2,1)S(1)}, u32[]{:S(2)}, u32[]{:S(2)}) async-start(bf16[16,2,40,512]{3,2,1,0:T(8,128)(2,1)} %shard_map.91), calls=%async_computation | async-start | bytes 2621440 | tf_op jit(solution)/shard_map/all_to_all | solution.py:291
  89.3 33.2 %collective-permute-start.6 = (bf16[1024,256]{1,0:T(8,128)(2,1)S(1)}, bf16[1024,256]{1,0:T(8,128)(2,1)S(1)}, u32[]{:S(2)}, u32[]{:S(2)}) collective-permute-start(bf16[1024,256]{1,0:T(8,128)(2,1)S(1)} %get-tuple-element.16), channel_id=1, source_target_pairs={{29,0},{30,1},{31,2},{0,3},{1,4},{2,5},{3,6},{4,7},{5,8},{6,9},{7,... | collective-permute-start | bytes 1572872 | tf_op jit(solution)/shard_map/ppermute | solution.py:26
  110.7 29.0 %all-to-all-start.1 = ((bf16[32,16,128]{2,1,0:T(8,128)(2,1)}), bf16[32,16,128]{2,1,0:T(8,128)(2,1)S(1)}, u32[]{:S(2)}, u32[]{:S(2)}) async-start(bf16[32,16,128]{2,1,0:T(8,128)(2,1)} %shard_map.92), calls=%async_computation.1 | async-start | bytes 262144 | tf_op jit(solution)/shard_map/all_to_all | solution.py:307

commit v4 on v3

--- a/solution.py
+++ b/solution.py
@@ -163,7 +163,7 @@
             sent_ref[part, layer] = lines[part * share : (part + 1) * share].astype(jnp.bfloat16)
 
 
-def stage_kernel(received_ref, _, sent_ref, flat, slots):
+def stage_kernel(received_ref, sent_ref, flat, slots):
     devices, layers, rows, width = received_ref.shape
     members, slot, _ = sent_ref.shape
     across = width // LANES
@@ -181,28 +181,33 @@
         sent_ref[i] = slots[i * slot : (i + 1) * slot].astype(jnp.bfloat16)
 
 
-def finish_kernel(received_ref, sums_ref):
-    sums_ref[...] = jnp.sum(received_ref[...].astype(jnp.float32), axis=0)
-
-
-def copy_kernel(from_ref, to_ref):
-    to_ref[...] = from_ref[...]
-
-
-def add_kernel(direct_ref, back_ref, grad_ref):
+def finish_kernel(received_ref, first_ref, second_ref):
+    sums = jnp.sum(received_ref[...].astype(jnp.float32), axis=0)
+    share = first_ref.shape[0] // LANES
+    for layer, out_ref in enumerate((first_ref, second_ref)):
+        for i in range(share):
+            out_ref[pl.ds(i * LANES, LANES)] = sums[layer * share + i]
+
+
+def copy_kernel(*refs):
+    half = len(refs) // 2
+    for from_ref, to_ref in zip(refs[:half], refs[half:]):
+        to_ref[...] = from_ref[...]
+
+
+def add_kernel(back_ref, direct_ref, grad_ref):
     grad_ref[...] = (
         direct_ref[...].astype(jnp.float32) + back_ref[...].astype(jnp.float32)
     ).astype(jnp.bfloat16)
 
 
-def call(kernel, outs, *args, scratch=(), flops=0, after=0):
+def call(kernel, outs, *args, scratch=(), flops=0):
     moved = sum(a.size * a.dtype.itemsize for a in (*args, *outs))
     here = pl.BlockSpec(memory_space=pltpu.VMEM)
-    waited = [pl.BlockSpec(memory_space=pl.ANY)] * after
     return pl.pallas_call(
         kernel,
         out_shape=tuple(outs),
-        in_specs=[here] * (len(args) - after) + waited,
+        in_specs=[here] * len(args),
         out_specs=(here,) * len(outs),
         scratch_shapes=list(scratch),
         compiler_params=pltpu.CompilerParams(vmem_limit_bytes=VMEM_LIMIT),
@@ -237,6 +242,10 @@
     x = move(x, homes)
     cot = move(cot, homes)
     cot_ahead = move(cot, [(place(i), place(j)) for i, j in pairs(-far)])
+    weights = (conv_first, proj_first, conv_second, proj_second)
+    conv_first, proj_first, conv_second, proj_second = call(
+        copy_kernel, [array(w.shape, w.dtype) for w in weights], *weights
+    )
     (own,) = call(
         prepare_kernel, (double,), x, conv_first, flops=4 * rows * channels * channels
     )
@@ -269,8 +278,8 @@
         proj_second,
         flops=38 * rows * channels * channels,
     )
+    direct = move(direct, [(j, i) for i, j in homes])
     tap_back = move(tap, [(place(j), i) for i, j in pairs(near)])
-    direct = move(direct, [(j, i) for i, j in homes])
     weight_rows = 2 * channels + channels * channels // width
     (sent,) = call(
         functools.partial(weights_kernel, scale),
@@ -291,26 +300,20 @@
     received = lax.all_to_all(sent, ("dp", "group"), 0, 0, tiled=True)
     share = weight_rows * width // (parts * members * LANES)
     slot = -(-2 * share // 16) * 16
-    (tap_back,) = call(copy_kernel, (narrow,), tap_back, flops=BESIDE)
-    (grad_x,) = call(add_kernel, (narrow,), direct, tap_back, flops=BESIDE)
+    (grad_x,) = call(add_kernel, (narrow,), tap_back, direct)
     (sent,) = call(
         stage_kernel,
         (array((members, slot, LANES), bf16),),
         received,
-        tap_back,
         scratch=[
             pltpu.VMEM((members * share, LANES), f32),
             pltpu.VMEM((members * slot, LANES), f32),
         ],
-        after=1,
     )
     received = lax.all_to_all(sent, "member", 0, 0, tiled=True)
-    (sums,) = call(finish_kernel, (array((slot, LANES), f32),), received)
-    return (
-        grad_x.reshape(shape),
-        sums[:share].reshape(-1),
-        sums[share : 2 * share].reshape(-1),
-    )
+    own_share = array((share * LANES,), f32)
+    sums_first, sums_second = call(finish_kernel, (own_share, own_share), received)
+    return grad_x.reshape(shape), sums_first, sums_second
 
 
 def solution(mesh):

time: 141 us -> 135 us (0.957); the launches traced: 140 us -> 133 us
  waiting for transfers between devices: 72.5 us -> 64.6 us
  starting transfers between devices: 56 us -> 53.4 us
  local copies, waits for them, and re-layouts: 1.67 us -> 3.88 us
    all_to_all x1, waiting for transfers between devices: 16.3 us -> 7.76 us  [per_device(): received = lax.all_to_all(sent, 'member', 0, 0, tiled=True)]
    all_to_all x1, waiting for transfers between devices: 4.52 us -> 11.8 us  [per_device(): received = lax.all_to_all(sent, ('dp', 'group'), 0, 0, tiled=True)]
    ppermute x8, waiting for transfers between devices: 51.6 us -> 45.1 us  [move(): return lax.ppermute(block, ('group', 'member'), route)]
    unnamed x10 -> x8, local copies, waits for them, and re-layouts: 1.06 us -> 3.88 us
    all_to_all x1, starting transfers between devices: 11.8 us -> 9.27 us  [per_device(): received = lax.all_to_all(sent, 'member', 0, 0, tiled=True)]
  transfers between devices with their start and end apart: 10 -> 10, of which waited for: 8 -> 8; matrix products, arithmetic and copies ran while one was open for 0% -> 0% of each run, Pallas kernels for 4% -> 3%
where the time goes in v4:
time: 135 us; the launch traced here: 133 us
  waiting for transfers between devices  64.6 us (48%)
  starting transfers between devices  53.4 us (40%)
  Pallas kernels  10.1 us (7%)
  local copies, waits for them, and re-layouts  3.88 us (3%)
    ppermute x8, waiting for transfers between devices, move(): return lax.ppermute(block, ('group', 'member'), route)  45.1 us
    ppermute x8, starting transfers between devices, move(): return lax.ppermute(block, ('group', 'member'), route)  36.1 us
    all_to_all x1, waiting for transfers between devices, per_device(): received = lax.all_to_all(sent, ('dp', 'group'), 0, 0, tiled=True)  11.8 us
    pallas_call x9, Pallas kernels, call(): pl.pallas_call(kernel, out_shape=tuple(outs), in_specs=[here] * len(args)...  10.1 us
    all_to_all x1, starting transfers between devices, per_device(): received = lax.all_to_all(sent, 'member', 0, 0, tiled=True)  9.27 us
    all_to_all x1, starting transfers between devices, per_device(): received = lax.all_to_all(sent, ('dp', 'group'), 0, 0, tiled=True)  7.95 us
    all_to_all x1, waiting for transfers between devices, per_device(): received = lax.all_to_all(sent, 'member', 0, 0, tiled=True)  7.76 us
    unnamed x8, local copies, waits for them, and re-layouts  3.88 us
  transfers between devices with their start and end apart: 10, of which 8 were waited for; matrix products, arithmetic and copies ran while one was open for 0% of the time, Pallas kernels for 3%

profile of v4, /device:TPU:6, one launch (start us, length us, event | category | flops | bytes accessed | tf_op | source)
XLA Modules:
  0.0 132.7 jit_solution(11080547540409567909)
XLA Ops:
  0.6 11.3 %collective-permute-start.4 = (bf16[1024,256]{1,0:T(8,128)(2,1)}, bf16[1024,256]{1,0:T(8,128)(2,1)S(1)}, u32[]{:S(2)}, u32[]{:S(2)}) collective-permute-start(bf16[1024,256]{1,0:T(8,128)(2,1)} %bitcast.4), channel_id=1, source_target_pairs={{0,29},{1,30},{2,31},{3,0},{4,1},{5,2},{6,3},{7,4},{8,5},{9,6},{10... | collective-permute-start | bytes 1572872 | tf_op jit(solution)/shard_map/ppermute | solution.py:26
  11.9 3.2 %collective-permute-start = (bf16[1024,256]{1,0:T(8,128)(2,1)}, bf16[1024,256]{1,0:T(8,128)(2,1)S(1)}, u32[]{:S(2)}, u32[]{:S(2)}) collective-permute-start(bf16[1024,256]{1,0:T(8,128)(2,1)} %bitcast.5), channel_id=1, source_target_pairs={{0,29},{1,30},{2,31},{3,0},{4,1},{5,2},{6,3},{7,4},{8,5},{9,6},{10... | collective-permute-start | bytes 1572872 | tf_op jit(solution)/shard_map/ppermute | solution.py:26
  15.1 2.8 %collective-permute-start.1 = (bf16[1024,256]{1,0:T(8,128)(2,1)}, bf16[1024,256]{1,0:T(8,128)(2,1)S(1)}, u32[]{:S(2)}, u32[]{:S(2)}) collective-permute-start(bf16[1024,256]{1,0:T(8,128)(2,1)} %bitcast.6), channel_id=1, source_target_pairs={{0,5},{1,6},{2,7},{3,8},{4,9},{5,10},{6,11},{7,12},{8,13},{9,14},{... | collective-permute-start | bytes 1572872 | tf_op jit(solution)/shard_map/ppermute | solution.py:26
  18.0 12.8 %collective-permute-done.4.cot_ref.refs_9_ = bf16[1024,256]{1,0:T(8,128)(2,1)S(1)} collective-permute-done((bf16[1024,256]{1,0:T(8,128)(2,1)}, bf16[1024,256]{1,0:T(8,128)(2,1)S(1)}, u32[]{:S(2)}, u32[]{:S(2)}) %collective-permute-start.4) | collective-permute-done | bytes 524320 | tf_op jit(solution)/shard_map/ppermute | solution.py:26
  30.7 2.7 %collective-permute-start.5 = (bf16[1024,256]{1,0:T(8,128)(2,1)S(1)}, bf16[1024,256]{1,0:T(8,128)(2,1)S(1)}, u32[]{:S(2)}, u32[]{:S(2)}) collective-permute-start(bf16[1024,256]{1,0:T(8,128)(2,1)S(1)} %collective-permute-done.4.cot_ref.refs_9_), channel_id=1, source_target_pairs={{61,29},{62,30},{63,31},{32,0},{33,1},{34,2},{35,3},{36,4},{37,5},... | collective-permute-start | bytes 1572872 | tf_op jit(solution)/shard_map/ppermute | solution.py:26
  33.4 0.0 copy-start
  33.5 1.0 copy-done
  34.5 0.0 copy-start.1
  34.5 1.0 copy-done.1
  35.5 0.0 copy-start.2
  35.5 0.9 copy-done.2
  36.4 0.0 copy-start.3
  36.4 0.9 copy-done.3
  37.3 0.1 shard_map.85
  37.4 9.1 %collective-permute-done.x_ref.refs_1_ = bf16[1024,256]{1,0:T(8,128)(2,1)S(1)} collective-permute-done((bf16[1024,256]{1,0:T(8,128)(2,1)}, bf16[1024,256]{1,0:T(8,128)(2,1)S(1)}, u32[]{:S(2)}, u32[]{:S(2)}) %collective-permute-start) | collective-permute-done | bytes 524320 | tf_op jit(solution)/shard_map/ppermute | solution.py:26
  46.5 0.4 shard_map.86.own_ref
  47.0 3.6 %collective-permute-done.1.past_ref.refs_0_ = bf16[1024,256]{1,0:T(8,128)(2,1)S(1)} collective-permute-done((bf16[1024,256]{1,0:T(8,128)(2,1)}, bf16[1024,256]{1,0:T(8,128)(2,1)S(1)}, u32[]{:S(2)}, u32[]{:S(2)}) %collective-permute-start.1) | collective-permute-done | bytes 524320 | tf_op jit(solution)/shard_map/ppermute | solution.py:26
  50.6 0.7 shard_map.87
  51.3 2.7 %collective-permute-start.3 = (bf16[1024,256]{1,0:T(8,128)(2,1)S(1)}, bf16[1024,256]{1,0:T(8,128)(2,1)S(1)}, u32[]{:S(2)}, u32[]{:S(2)}) collective-permute-start(bf16[1024,256]{1,0:T(8,128)(2,1)S(1)} %get-tuple-element.21.middle_ref.refs_6_), channel_id=1, source_target_pairs={{61,29},{62,30},{63,31},{32,0},{33,1},{34,2},{35,3},{36,4},{37,5},... | collective-permute-start | bytes 1572872 | tf_op jit(solution)/shard_map/ppermute | solution.py:26
  54.0 7.7 %collective-permute-start.2 = (bf16[1024,256]{1,0:T(8,128)(2,1)S(1)}, bf16[1024,256]{1,0:T(8,128)(2,1)S(1)}, u32[]{:S(2)}, u32[]{:S(2)}) collective-permute-start(bf16[1024,256]{1,0:T(8,128)(2,1)S(1)} %get-tuple-element.21.middle_ref.refs_6_), channel_id=1, source_target_pairs={{29,61},{30,62},{31,63},{0,32},{1,33},{2,34},{3,35},{4,36},{5,37},... | collective-permute-start | bytes 1572872 | tf_op jit(solution)/shard_map/ppermute | solution.py:26
  61.8 0.0 collective-permute-done.5.cot_ref
  61.8 0.3 shard_map.88.gated_ahead_ref
  62.1 9.9 %collective-permute-done.3.middle_ahead_ref = bf16[1024,256]{1,0:T(8,128)(2,1)S(1)} collective-permute-done((bf16[1024,256]{1,0:T(8,128)(2,1)S(1)}, bf16[1024,256]{1,0:T(8,128)(2,1)S(1)}, u32[]{:S(2)}, u32[]{:S(2)}) %collective-permute-start.3) | collective-permute-done | bytes 524320 | tf_op jit(solution)/shard_map/ppermute | solution.py:26
  72.0 1.2 collective-permute-done.2.middle_past_ref.refs_5_
  73.2 3.4 %shard_map.89 = (bf16[1024,256]{1,0:T(8,128)(2,1)S(1)}, bf16[1024,256]{1,0:T(8,128)(2,1)S(1)}, bf16[1024,256]{1,0:T(8,128)(2,1)S(1)}, bf16[1024,512]{1,0:T(8,128...) custom-call(bf16[1024,256]{1,0:T(8,128)(2,1)S(1)} %get-tuple-element.21.middle_ref.refs_6_, ...), custom_call_target="tpu_custom_call" | custom-call | flops 2550136832 | bytes 10747904 | tf_op jit(solution)/shard_map/pallas_call | solution.py:207
  76.6 2.7 %shard_map.91 = bf16[16,2,40,512]{3,2,1,0:T(8,128)(2,1)} custom-call(bf16[1024,256]{1,0:T(8,128)(2,1)S(1)} %collective-permute-done.1.past_ref.refs_0_, bf16[1024,256]{1,0:T(8,128)(2,1)S(1)} %collective-permute-done.x_ref.refs_1_, bf16[1024,512]{1,0:T(8,128)(2,1)S(1)} %get-tuple-element.28.refs_2_, bf16[1024,256]{1,0:T(8,128)(2,1)S(1)} %get-tuple-element.29.refs_3_, ...), custom_call_target="tpu_custom_call" | custom-call | flops 1342177280 | bytes 7602176 | tf_op jit(solution)/shard_map/pallas_call | solution.py:207
  79.3 7.9 %all-to-all-start = ((bf16[16,2,40,512]{3,2,1,0:T(8,128)(2,1)}), bf16[16,2,40,512]{3,2,1,0:T(8,128)(2,1)S(1)}, u32[]{:S(2)}, u32[]{:S(2)}) async-start(bf16[16,2,40,512]{3,2,1,0:T(8,128)(2,1)} %shard_map.91), calls=%async_computation | async-start | bytes 2621440 | tf_op jit(solution)/shard_map/all_to_all | solution.py:300
  87.2 1.9 %collective-permute-start.6 = (bf16[1024,256]{1,0:T(8,128)(2,1)S(1)}, bf16[1024,256]{1,0:T(8,128)(2,1)S(1)}, u32[]{:S(2)}, u32[]{:S(2)}) collective-permute-start(bf16[1024,256]{1,0:T(8,128)(2,1)S(1)} %get-tuple-element.26), channel_id=1, source_target_pairs={{5,0},{6,1},{7,2},{8,3},{9,4},{10,5},{11,6},{12,7},{13,8},{14,9},{... | collective-permute-start | bytes 1572872 | tf_op jit(solution)/shard_map/ppermute | solution.py:26
  89.1 3.7 %collective-permute-start.7 = (bf16[1024,256]{1,0:T(8,128)(2,1)S(1)}, bf16[1024,256]{1,0:T(8,128)(2,1)S(1)}, u32[]{:S(2)}, u32[]{:S(2)}) collective-permute-start(bf16[1024,256]{1,0:T(8,128)(2,1)S(1)} %get-tuple-element.27), channel_id=1, source_target_pairs={{29,0},{30,1},{31,2},{0,3},{1,4},{2,5},{3,6},{4,7},{5,8},{6,9},{7,... | collective-permute-start | bytes 1572872 | tf_op jit(solution)/shard_map/ppermute | solution.py:26
  92.9 11.8 %all-to-all-done.received_ref = bf16[16,2,40,512]{3,2,1,0:T(8,128)(2,1)S(1)} async-done(((bf16[16,2,40,512]{3,2,1,0:T(8,128)(2,1)}), bf16[16,2,40,512]{3,2,1,0:T(8,128)(2,1)S(1)}, u32[]{:S(2)}, u32[]{:S(2)}) %all-to-all-start) | async-done | bytes 1310752 | tf_op jit(solution)/shard_map/all_to_all | solution.py:300
  104.6 0.9 shard_map.92
  105.6 9.3 %all-to-all-start.1 = ((bf16[32,16,128]{2,1,0:T(8,128)(2,1)}), bf16[32,16,128]{2,1,0:T(8,128)(2,1)S(1)}, u32[]{:S(2)}, u32[]{:S(2)}) async-start(bf16[32,16,128]{2,1,0:T(8,128)(2,1)} %shard_map.92), calls=%async_computation.1 | async-start | bytes 262144 | tf_op jit(solution)/shard_map/all_to_all | solution.py:313
  114.9 8.5 %collective-permute-done.6.back_ref = bf16[1024,256]{1,0:T(8,128)(2,1)S(1)} collective-permute-done((bf16[1024,256]{1,0:T(8,128)(2,1)S(1)}, bf16[1024,256]{1,0:T(8,128)(2,1)S(1)}, u32[]{:S(2)}, u32[]{:S(2)}) %collective-permute-start.6) | collective-permute-done | bytes 524320 | tf_op jit(solution)/shard_map/ppermute | solution.py:26
  123.4 0.0 collective-permute-done.7.direct_ref
  123.4 0.9 shard_map.90
  124.3 7.8 %all-to-all-done.1.received_ref = bf16[32,16,128]{2,1,0:T(8,128)(2,1)S(1)} async-done(((bf16[32,16,128]{2,1,0:T(8,128)(2,1)}), bf16[32,16,128]{2,1,0:T(8,128)(2,1)S(1)}, u32[]{:S(2)}, u32[]{:S(2)}) %all-to-all-start.1) | async-done | bytes 131104 | tf_op jit(solution)/shard_map/all_to_all | solution.py:313
  132.1 0.6 shard_map.93
Async XLA Ops:
  0.6 30.1 %collective-permute-start.4 = (bf16[1024,256]{1,0:T(8,128)(2,1)}, bf16[1024,256]{1,0:T(8,128)(2,1)S(1)}, u32[]{:S(2)}, u32[]{:S(2)}) collective-permute-start(bf16[1024,256]{1,0:T(8,128)(2,1)} %bitcast.4), channel_id=1, source_target_pairs={{0,29},{1,30},{2,31},{3,0},{4,1},{5,2},{6,3},{7,4},{8,5},{9,6},{10... | collective-permute-start | bytes 1572872 | tf_op jit(solution)/shard_map/ppermute | solution.py:26
  11.9 34.6 %collective-permute-start = (bf16[1024,256]{1,0:T(8,128)(2,1)}, bf16[1024,256]{1,0:T(8,128)(2,1)S(1)}, u32[]{:S(2)}, u32[]{:S(2)}) collective-permute-start(bf16[1024,256]{1,0:T(8,128)(2,1)} %bitcast.5), channel_id=1, source_target_pairs={{0,29},{1,30},{2,31},{3,0},{4,1},{5,2},{6,3},{7,4},{8,5},{9,6},{10... | collective-permute-start | bytes 1572872 | tf_op jit(solution)/shard_map/ppermute | solution.py:26
  15.1 35.4 %collective-permute-start.1 = (bf16[1024,256]{1,0:T(8,128)(2,1)}, bf16[1024,256]{1,0:T(8,128)(2,1)S(1)}, u32[]{:S(2)}, u32[]{:S(2)}) collective-permute-start(bf16[1024,256]{1,0:T(8,128)(2,1)} %bitcast.6), channel_id=1, source_target_pairs={{0,5},{1,6},{2,7},{3,8},{4,9},{5,10},{6,11},{7,12},{8,13},{9,14},{... | collective-permute-start | bytes 1572872 | tf_op jit(solution)/shard_map/ppermute | solution.py:26
  30.7 31.1 %collective-permute-start.5 = (bf16[1024,256]{1,0:T(8,128)(2,1)S(1)}, bf16[1024,256]{1,0:T(8,128)(2,1)S(1)}, u32[]{:S(2)}, u32[]{:S(2)}) collective-permute-start(bf16[1024,256]{1,0:T(8,128)(2,1)S(1)} %collective-permute-done.4.cot_ref.refs_9_), channel_id=1, source_target_pairs={{61,29},{62,30},{63,31},{32,0},{33,1},{34,2},{35,3},{36,4},{37,5},... | collective-permute-start | bytes 1572872 | tf_op jit(solution)/shard_map/ppermute | solution.py:26
  33.4 1.0 copy-start
  34.5 1.0 copy-start.1
  35.5 0.9 copy-start.2
  36.4 0.9 copy-start.3
  51.3 20.8 %collective-permute-start.3 = (bf16[1024,256]{1,0:T(8,128)(2,1)S(1)}, bf16[1024,256]{1,0:T(8,128)(2,1)S(1)}, u32[]{:S(2)}, u32[]{:S(2)}) collective-permute-start(bf16[1024,256]{1,0:T(8,128)(2,1)S(1)} %get-tuple-element.21.middle_ref.refs_6_), channel_id=1, source_target_pairs={{61,29},{62,30},{63,31},{32,0},{33,1},{34,2},{35,3},{36,4},{37,5},... | collective-permute-start | bytes 1572872 | tf_op jit(solution)/shard_map/ppermute | solution.py:26
  54.0 19.2 %collective-permute-start.2 = (bf16[1024,256]{1,0:T(8,128)(2,1)S(1)}, bf16[1024,256]{1,0:T(8,128)(2,1)S(1)}, u32[]{:S(2)}, u32[]{:S(2)}) collective-permute-start(bf16[1024,256]{1,0:T(8,128)(2,1)S(1)} %get-tuple-element.21.middle_ref.refs_6_), channel_id=1, source_target_pairs={{29,61},{30,62},{31,63},{0,32},{1,33},{2,34},{3,35},{4,36},{5,37},... | collective-permute-start | bytes 1572872 | tf_op jit(solution)/shard_map/ppermute | solution.py:26
  79.3 25.4 %all-to-all-start = ((bf16[16,2,40,512]{3,2,1,0:T(8,128)(2,1)}), bf16[16,2,40,512]{3,2,1,0:T(8,128)(2,1)S(1)}, u32[]{:S(2)}, u32[]{:S(2)}) async-start(bf16[16,2,40,512]{3,2,1,0:T(8,128)(2,1)} %shard_map.91), calls=%async_computation | async-start | bytes 2621440 | tf_op jit(solution)/shard_map/all_to_all | solution.py:300
  87.2 36.2 %collective-permute-start.6 = (bf16[1024,256]{1,0:T(8,128)(2,1)S(1)}, bf16[1024,256]{1,0:T(8,128)(2,1)S(1)}, u32[]{:S(2)}, u32[]{:S(2)}) collective-permute-start(bf16[1024,256]{1,0:T(8,128)(2,1)S(1)} %get-tuple-element.26), channel_id=1, source_target_pairs={{5,0},{6,1},{7,2},{8,3},{9,4},{10,5},{11,6},{12,7},{13,8},{14,9},{... | collective-permute-start | bytes 1572872 | tf_op jit(solution)/shard_map/ppermute | solution.py:26
  89.1 34.3 %collective-permute-start.7 = (bf16[1024,256]{1,0:T(8,128)(2,1)S(1)}, bf16[1024,256]{1,0:T(8,128)(2,1)S(1)}, u32[]{:S(2)}, u32[]{:S(2)}) collective-permute-start(bf16[1024,256]{1,0:T(8,128)(2,1)S(1)} %get-tuple-element.27), channel_id=1, source_target_pairs={{29,0},{30,1},{31,2},{0,3},{1,4},{2,5},{3,6},{4,7},{5,8},{6,9},{7,... | collective-permute-start | bytes 1572872 | tf_op jit(solution)/shard_map/ppermute | solution.py:26
  105.6 26.5 %all-to-all-start.1 = ((bf16[32,16,128]{2,1,0:T(8,128)(2,1)}), bf16[32,16,128]{2,1,0:T(8,128)(2,1)S(1)}, u32[]{:S(2)}, u32[]{:S(2)}) async-start(bf16[32,16,128]{2,1,0:T(8,128)(2,1)} %shard_map.92), calls=%async_computation.1 | async-start | bytes 262144 | tf_op jit(solution)/shard_map/all_to_all | solution.py:313

commit v5 on v4

--- a/solution.py
+++ b/solution.py
@@ -13,17 +13,18 @@
 BESIDE = 2 * 10**10
 VMEM_LIMIT = 16 * 1024 * 1024
 LANES = 128
+BLOCKS = ("group", "ring", "core")
 
 
 def split_axes(mesh):
     blocks = mesh.devices.shape[1]
-    member = min(32, blocks // 2)
-    split = mesh.devices.reshape(mesh.devices.shape[0], blocks // member, member)
-    return Mesh(split, ("dp", "group", "member"))
+    ring = min(16, blocks // 4)
+    split = mesh.devices.reshape(mesh.devices.shape[0], blocks // (2 * ring), ring, 2)
+    return Mesh(split, ("dp", *BLOCKS))
 
 
 def move(block, route):
-    return lax.ppermute(block, ("group", "member"), route)
+    return lax.ppermute(block, BLOCKS, route)
 
 
 def contract_rows(left, right):
@@ -93,12 +94,18 @@
         ).astype(jnp.bfloat16)
 
 
+def tap_kernel(middle_ref, middle_ahead_ref, gated_ahead_ref, conv_ref, tap_ref):
+    for part in tiles(middle_ref.shape[0]):
+        t, s = gates(middle_ahead_ref[part], middle_ref[part], conv_ref)
+        ahead = gate_gradient(t, s, gated_ahead_ref[part])
+        tap_ref[part] = contract_cols(ahead, conv_ref[0]).astype(jnp.bfloat16)
+
+
 def backward_kernel(
     middle_ref,
     middle_past_ref,
-    middle_ahead_ref,
+    tap_second_ref,
     cot_ref,
-    gated_ahead_ref,
     tanh_ref,
     sig_ref,
     conv_first_ref,
@@ -114,9 +121,6 @@
 ):
     for part in tiles(middle_ref.shape[0]):
         middle, cot = middle_ref[part], cot_ref[part]
-        t, s = gates(middle_ahead_ref[part], middle, conv_second_ref)
-        ahead = gate_gradient(t, s, gated_ahead_ref[part])
-        back = contract_cols(ahead, conv_second_ref[0]).astype(jnp.bfloat16)
         t, s = gates(middle, middle_past_ref[part], conv_second_ref)
         gated_second_ref[part] = (t * s).astype(jnp.bfloat16)
         here = gate_gradient(t, s, contract_cols(cot, proj_second_ref[...]))
@@ -124,7 +128,7 @@
         grad = (
             cot.astype(jnp.float32)
             + contract_cols(here, conv_second_ref[1])
-            + back.astype(jnp.float32)
+            + tap_second_ref[part].astype(jnp.float32)
         ).astype(jnp.bfloat16)
         grad_ref[part] = grad
         here = gate_gradient(
@@ -137,47 +141,40 @@
         ).astype(jnp.bfloat16)
 
 
-def weights_kernel(scale, *refs):
-    inputs, (sent_ref, lines, square) = refs[:-3], refs[-3:]
-
-    def total(left, right):
-        return contract_rows(left[...], right[...]) * scale
-
-    share = sent_ref.shape[2]
+def weights_kernel(scale, ring, *refs):
+    inputs, (sent_ref, flat) = refs[:-2], refs[-2:]
+    devices, _, rows, _ = sent_ref.shape
+    share = rows // ring
+
+    def put(start, left, right):
+        total = contract_rows(left[...], right[...]) * scale
+        inner, across = total.shape[0], total.shape[1] // LANES
+        for i in range(across):
+            flat[pl.ds(start + i, inner, stride=across)] = total[:, i * LANES : (i + 1) * LANES]
+        return start + inner * across
+
     for layer in range(2):
         past, current, pre, gated, grad = inputs[layer * 5 : layer * 5 + 5]
-        inner, width = past.shape[1], pre.shape[1]
-        lines[:inner] = total(past, pre)
-        lines[inner : 2 * inner] = total(current, pre)
-        proj = total(gated, grad)
-        columns = proj.shape[1]
-        per_line = width // columns
-        for i in range(columns // LANES):
-            square[...] = proj[:, i * LANES : (i + 1) * LANES]
-            for j in range(per_line):
-                at = j * columns + i * LANES
-                lines[2 * inner :, at : at + LANES] = square[
-                    pl.ds(j, inner // per_line, stride=per_line)
-                ]
-        for part in range(sent_ref.shape[0]):
-            sent_ref[part, layer] = lines[part * share : (part + 1) * share].astype(jnp.bfloat16)
-
-
-def stage_kernel(received_ref, sent_ref, flat, slots):
-    devices, layers, rows, width = received_ref.shape
-    members, slot, _ = sent_ref.shape
-    across = width // LANES
-    share = rows * across // members
+        put(put(put(0, past, pre), current, pre), gated, grad)
+        for device in range(devices):
+            group, core = divmod(device, 2)
+            for j in range(share):
+                start = (group * ring * 2 + core) * share + j
+                sent_ref[device, layer, j * ring : (j + 1) * ring] = flat[
+                    pl.ds(start, ring, stride=2 * share)
+                ].astype(jnp.bfloat16)
+
+
+def stage_kernel(received_ref, sent_ref, slots):
+    _, layers, rows, _ = received_ref.shape
+    ring, slot, _ = sent_ref.shape
+    share = rows // ring
     slots[...] = jnp.zeros_like(slots)
     for layer in range(layers):
         total = jnp.sum(received_ref[:, layer].astype(jnp.float32), axis=0)
-        for i in range(across):
-            flat[pl.ds(i, rows, stride=across)] = total[:, i * LANES : (i + 1) * LANES]
         for j in range(share):
-            slots[pl.ds(layer * share + j, members, stride=slot)] = flat[
-                pl.ds(j, members, stride=share)
-            ]
-    for i in range(members):
+            slots[pl.ds(layer * share + j, ring, stride=slot)] = total[j * ring : (j + 1) * ring]
+    for i in range(ring):
         sent_ref[i] = slots[i * slot : (i + 1) * slot].astype(jnp.bfloat16)
 
 
@@ -219,9 +216,10 @@
     shape = x.shape
     channels, width = shape[2], conv_first.shape[2]
     rows = shape[0] * shape[1]
-    parts = lax.axis_size("dp") * lax.axis_size("group")
-    members = lax.axis_size("member")
+    ring = lax.axis_size("ring")
+    members = 2 * ring
     blocks = lax.axis_size("group") * members
+    plane = lax.axis_size("dp") * lax.axis_size("group") * 2
     near = min(8, blocks // 16)
     far = min(32, blocks // 4)
     scale = float(rows * lax.axis_size("dp") * blocks) ** (-0.5)
@@ -262,28 +260,37 @@
     )
     middle_past = move(middle, [(place(i), place(j)) for i, j in pairs(far)])
     middle_ahead = move(middle, [(place(i), place(j)) for i, j in pairs(-far)])
+    (tap_second,) = call(
+        tap_kernel,
+        (narrow,),
+        middle,
+        middle_ahead,
+        gated_ahead,
+        conv_second,
+        flops=12 * rows * channels * channels,
+    )
     tap, direct, gated_second, pre_second, grad, pre_first = call(
         backward_kernel,
         (narrow, narrow, narrow, wide, narrow, wide),
         middle,
         middle_past,
-        middle_ahead,
+        tap_second,
         cot,
-        gated_ahead,
         tanh_part,
         sig_part,
         conv_first,
         proj_first,
         conv_second,
         proj_second,
-        flops=38 * rows * channels * channels,
+        flops=26 * rows * channels * channels,
     )
     direct = move(direct, [(j, i) for i, j in homes])
     tap_back = move(tap, [(place(j), i) for i, j in pairs(near)])
-    weight_rows = 2 * channels + channels * channels // width
+    units = (2 * channels * width + channels * channels) // LANES
+    share = units // (plane * ring)
     (sent,) = call(
-        functools.partial(weights_kernel, scale),
-        (array((parts, 2, weight_rows // parts, width), bf16),),
+        functools.partial(weights_kernel, scale, ring),
+        (array((plane, 2, ring * share, LANES), bf16),),
         past,
         x,
         pre_first,
@@ -294,30 +301,26 @@
         pre_second,
         gated_second,
         cot,
-        scratch=[pltpu.VMEM((weight_rows, width), f32), pltpu.VMEM((channels, LANES), f32)],
+        scratch=[pltpu.VMEM((units, LANES), f32)],
         flops=rows * channels * 20 * channels,
     )
-    received = lax.all_to_all(sent, ("dp", "group"), 0, 0, tiled=True)
-    share = weight_rows * width // (parts * members * LANES)
+    received = lax.all_to_all(sent, ("dp", "group", "core"), 0, 0, tiled=True)
     slot = -(-2 * share // 16) * 16
-    (grad_x,) = call(add_kernel, (narrow,), tap_back, direct)
     (sent,) = call(
         stage_kernel,
-        (array((members, slot, LANES), bf16),),
+        (array((ring, slot, LANES), bf16),),
         received,
-        scratch=[
-            pltpu.VMEM((members * share, LANES), f32),
-            pltpu.VMEM((members * slot, LANES), f32),
-        ],
-    )
-    received = lax.all_to_all(sent, "member", 0, 0, tiled=True)
+        scratch=[pltpu.VMEM((ring * slot, LANES), f32)],
+    )
+    received = lax.all_to_all(sent, "ring", 0, 0, tiled=True)
+    (grad_x,) = call(add_kernel, (narrow,), tap_back, direct)
     own_share = array((share * LANES,), f32)
     sums_first, sums_second = call(finish_kernel, (own_share, own_share), received)
     return grad_x.reshape(shape), sums_first, sums_second
 
 
 def solution(mesh):
-    time, flat = P("dp", ("group", "member"), None), P(("dp", "group", "member"))
+    time, flat = P("dp", BLOCKS, None), P(("dp", *BLOCKS))
     return jax.shard_map(
         per_device,
         mesh=split_axes(mesh),

time: 135 us -> 131 us (0.970)
  the two profiles are of different devices: /device:TPU:6 before, /device:TPU:2 now
where the time goes in v5:
time: 131 us; the launch traced here: 130 us
  waiting for transfers between devices  62.5 us (48%)
  starting transfers between devices  52.4 us (40%)
  Pallas kernels  10.5 us (8%)
  local copies, waits for them, and re-layouts  3.88 us (3%)
    ppermute x8, waiting for transfers between devices, move(): return lax.ppermute(block, BLOCKS, route)  37.3 us
    ppermute x8, starting transfers between devices, move(): return lax.ppermute(block, BLOCKS, route)  30.1 us
    all_to_all x1, waiting for transfers between devices, per_device(): received = lax.all_to_all(sent, ('dp', 'group', 'core'), 0, 0, tiled=True)  13.9 us
    all_to_all x1, starting transfers between devices, per_device(): received = lax.all_to_all(sent, ('dp', 'group', 'core'), 0, 0, tiled=True)  12.4 us
    all_to_all x1, waiting for transfers between devices, per_device(): received = lax.all_to_all(sent, 'ring', 0, 0, tiled=True)  11.4 us
    pallas_call x10, Pallas kernels, call(): pl.pallas_call(kernel, out_shape=tuple(outs), in_specs=[here] * len(args)...  10.5 us
    all_to_all x1, starting transfers between devices, per_device(): received = lax.all_to_all(sent, 'ring', 0, 0, tiled=True)  9.95 us
    unnamed x8, local copies, waits for them, and re-layouts  3.88 us
  transfers between devices with their start and end apart: 10, of which 8 were waited for; matrix products, arithmetic and copies ran while one was open for 0% of the time, Pallas kernels for 4%

profile of v5, /device:TPU:2, one launch (start us, length us, event | category | flops | bytes accessed | tf_op | source)
XLA Modules:
  0.0 130.2 jit_solution(13767204192255100987)
XLA Ops:
  0.6 11.3 %collective-permute-start.4 = (bf16[1024,256]{1,0:T(8,128)(2,1)}, bf16[1024,256]{1,0:T(8,128)(2,1)S(1)}, u32[]{:S(2)}, u32[]{:S(2)}) collective-permute-start(bf16[1024,256]{1,0:T(8,128)(2,1)} %bitcast.4), channel_id=1, source_target_pairs={{0,29},{1,30},{2,31},{3,0},{4,1},{5,2},{6,3},{7,4},{8,5},{9,6},{10... | collective-permute-start | bytes 1572872 | tf_op jit(solution)/shard_map/ppermute | solution.py:27
  11.9 3.2 %collective-permute-start = (bf16[1024,256]{1,0:T(8,128)(2,1)}, bf16[1024,256]{1,0:T(8,128)(2,1)S(1)}, u32[]{:S(2)}, u32[]{:S(2)}) collective-permute-start(bf16[1024,256]{1,0:T(8,128)(2,1)} %bitcast.5), channel_id=1, source_target_pairs={{0,29},{1,30},{2,31},{3,0},{4,1},{5,2},{6,3},{7,4},{8,5},{9,6},{10... | collective-permute-start | bytes 1572872 | tf_op jit(solution)/shard_map/ppermute | solution.py:27
  15.1 2.8 %collective-permute-start.1 = (bf16[1024,256]{1,0:T(8,128)(2,1)}, bf16[1024,256]{1,0:T(8,128)(2,1)S(1)}, u32[]{:S(2)}, u32[]{:S(2)}) collective-permute-start(bf16[1024,256]{1,0:T(8,128)(2,1)} %bitcast.6), channel_id=1, source_target_pairs={{0,5},{1,6},{2,7},{3,8},{4,9},{5,10},{6,11},{7,12},{8,13},{9,14},{... | collective-permute-start | bytes 1572872 | tf_op jit(solution)/shard_map/ppermute | solution.py:27
  18.0 12.8 %collective-permute-done.4.cot_ref.refs_9_ = bf16[1024,256]{1,0:T(8,128)(2,1)S(1)} collective-permute-done((bf16[1024,256]{1,0:T(8,128)(2,1)}, bf16[1024,256]{1,0:T(8,128)(2,1)S(1)}, u32[]{:S(2)}, u32[]{:S(2)}) %collective-permute-start.4) | collective-permute-done | bytes 524320 | tf_op jit(solution)/shard_map/ppermute | solution.py:27
  30.7 1.9 %collective-permute-start.5 = (bf16[1024,256]{1,0:T(8,128)(2,1)S(1)}, bf16[1024,256]{1,0:T(8,128)(2,1)S(1)}, u32[]{:S(2)}, u32[]{:S(2)}) collective-permute-start(bf16[1024,256]{1,0:T(8,128)(2,1)S(1)} %collective-permute-done.4.cot_ref.refs_9_), channel_id=1, source_target_pairs={{61,29},{62,30},{63,31},{32,0},{33,1},{34,2},{35,3},{36,4},{37,5},... | collective-permute-start | bytes 1572872 | tf_op jit(solution)/shard_map/ppermute | solution.py:27
  32.6 0.0 copy-start
  32.6 1.0 copy-done
  33.7 0.0 copy-start.1
  33.7 1.0 copy-done.1
  34.7 0.0 copy-start.2
  34.7 0.9 copy-done.2
  35.6 0.0 copy-start.3
  35.6 0.9 copy-done.3
  36.5 0.1 shard_map.85
  36.6 9.9 %collective-permute-done.x_ref.refs_1_ = bf16[1024,256]{1,0:T(8,128)(2,1)S(1)} collective-permute-done((bf16[1024,256]{1,0:T(8,128)(2,1)}, bf16[1024,256]{1,0:T(8,128)(2,1)S(1)}, u32[]{:S(2)}, u32[]{:S(2)}) %collective-permute-start) | collective-permute-done | bytes 524320 | tf_op jit(solution)/shard_map/ppermute | solution.py:27
  46.5 0.4 shard_map.86.own_ref
  47.0 3.6 %collective-permute-done.1.past_ref.refs_0_ = bf16[1024,256]{1,0:T(8,128)(2,1)S(1)} collective-permute-done((bf16[1024,256]{1,0:T(8,128)(2,1)}, bf16[1024,256]{1,0:T(8,128)(2,1)S(1)}, u32[]{:S(2)}, u32[]{:S(2)}) %collective-permute-start.1) | collective-permute-done | bytes 524320 | tf_op jit(solution)/shard_map/ppermute | solution.py:27
  50.6 0.7 shard_map.87
  51.3 1.9 %collective-permute-start.3 = (bf16[1024,256]{1,0:T(8,128)(2,1)S(1)}, bf16[1024,256]{1,0:T(8,128)(2,1)S(1)}, u32[]{:S(2)}, u32[]{:S(2)}) collective-permute-start(bf16[1024,256]{1,0:T(8,128)(2,1)S(1)} %get-tuple-element.21.middle_ref.refs_6_), channel_id=1, source_target_pairs={{61,29},{62,30},{63,31},{32,0},{33,1},{34,2},{35,3},{36,4},{37,5},... | collective-permute-start | bytes 1572872 | tf_op jit(solution)/shard_map/ppermute | solution.py:27
  53.2 3.9 %collective-permute-start.2 = (bf16[1024,256]{1,0:T(8,128)(2,1)S(1)}, bf16[1024,256]{1,0:T(8,128)(2,1)S(1)}, u32[]{:S(2)}, u32[]{:S(2)}) collective-permute-start(bf16[1024,256]{1,0:T(8,128)(2,1)S(1)} %get-tuple-element.21.middle_ref.refs_6_), channel_id=1, source_target_pairs={{29,61},{30,62},{31,63},{0,32},{1,33},{2,34},{3,35},{4,36},{5,37},... | collective-permute-start | bytes 1572872 | tf_op jit(solution)/shard_map/ppermute | solution.py:27
  57.1 0.0 collective-permute-done.5.cot_ref
  57.1 0.3 shard_map.88.gated_ahead_ref
  57.5 9.6 %collective-permute-done.3.middle_ahead_ref = bf16[1024,256]{1,0:T(8,128)(2,1)S(1)} collective-permute-done((bf16[1024,256]{1,0:T(8,128)(2,1)S(1)}, bf16[1024,256]{1,0:T(8,128)(2,1)S(1)}, u32[]{:S(2)}, u32[]{:S(2)}) %collective-permute-start.3) | collective-permute-done | bytes 524320 | tf_op jit(solution)/shard_map/ppermute | solution.py:27
  67.0 1.3 shard_map.89.tap_second_ref
  68.3 0.6 collective-permute-done.2.middle_past_ref.refs_5_
  69.0 2.5 %shard_map.90 = (bf16[1024,256]{1,0:T(8,128)(2,1)S(1)}, bf16[1024,256]{1,0:T(8,128)(2,1)S(1)}, bf16[1024,256]{1,0:T(8,128)(2,1)S(1)}, bf16[1024,512]{1,0:T(8,128...) custom-call(bf16[1024,256]{1,0:T(8,128)(2,1)S(1)} %get-tuple-element.21.middle_ref.refs_6_, ...), custom_call_target="tpu_custom_call" | custom-call | flops 1744830464 | bytes 9699328 | tf_op jit(solution)/shard_map/pallas_call | solution.py:204
  71.5 2.8 %shard_map.92 = bf16[32,2,80,128]{3,2,1,0:T(8,128)(2,1)} custom-call(bf16[1024,256]{1,0:T(8,128)(2,1)S(1)} %collective-permute-done.1.past_ref.refs_0_, bf16[1024,256]{1,0:T(8,128)(2,1)S(1)} %collective-permute-done.x_ref.refs_1_, bf16[1024,512]{1,0:T(8,128)(2,1)S(1)} %get-tuple-element.28.refs_2_, bf16[1024,256]{1,0:T(8,128)(2,1)S(1)} %get-tuple-element.29.refs_3_, ...), custom_call_target="tpu_custom_call" | custom-call | flops 1342177280 | bytes 7602176 | tf_op jit(solution)/shard_map/pallas_call | solution.py:204
  74.3 12.4 %all-to-all-start = ((bf16[32,2,80,128]{3,2,1,0:T(8,128)(2,1)}), bf16[32,2,80,128]{3,2,1,0:T(8,128)(2,1)S(1)}, u32[]{:S(2)}, u32[]{:S(2)}) async-start(bf16[32,2,80,128]{3,2,1,0:T(8,128)(2,1)} %shard_map.92), calls=%async_computation | async-start | bytes 2621440 | tf_op jit(solution)/shard_map/all_to_all | solution.py:307
  86.7 1.9 %collective-permute-start.6 = (bf16[1024,256]{1,0:T(8,128)(2,1)S(1)}, bf16[1024,256]{1,0:T(8,128)(2,1)S(1)}, u32[]{:S(2)}, u32[]{:S(2)}) collective-permute-start(bf16[1024,256]{1,0:T(8,128)(2,1)S(1)} %get-tuple-element.26), channel_id=1, source_target_pairs={{5,0},{6,1},{7,2},{8,3},{9,4},{10,5},{11,6},{12,7},{13,8},{14,9},{... | collective-permute-start | bytes 1572872 | tf_op jit(solution)/shard_map/ppermute | solution.py:27
  88.6 3.1 %collective-permute-start.7 = (bf16[1024,256]{1,0:T(8,128)(2,1)S(1)}, bf16[1024,256]{1,0:T(8,128)(2,1)S(1)}, u32[]{:S(2)}, u32[]{:S(2)}) collective-permute-start(bf16[1024,256]{1,0:T(8,128)(2,1)S(1)} %get-tuple-element.27), channel_id=1, source_target_pairs={{29,0},{30,1},{31,2},{0,3},{1,4},{2,5},{3,6},{4,7},{5,8},{6,9},{7,... | collective-permute-start | bytes 1572872 | tf_op jit(solution)/shard_map/ppermute | solution.py:27
  91.7 13.9 %all-to-all-done.received_ref = bf16[32,2,80,128]{3,2,1,0:T(8,128)(2,1)S(1)} async-done(((bf16[32,2,80,128]{3,2,1,0:T(8,128)(2,1)}), bf16[32,2,80,128]{3,2,1,0:T(8,128)(2,1)S(1)}, u32[]{:S(2)}, u32[]{:S(2)}) %all-to-all-start) | async-done | bytes 1310752 | tf_op jit(solution)/shard_map/all_to_all | solution.py:307
  105.6 0.9 shard_map.93
  106.5 10.0 %all-to-all-start.1 = ((bf16[16,16,128]{2,1,0:T(8,128)(2,1)}), bf16[16,16,128]{2,1,0:T(8,128)(2,1)S(1)}, u32[]{:S(2)}, u32[]{:S(2)}) async-start(bf16[16,16,128]{2,1,0:T(8,128)(2,1)} %shard_map.93), calls=%async_computation.1 | async-start | bytes 131072 | tf_op jit(solution)/shard_map/all_to_all | solution.py:315
  116.5 0.8 collective-permute-done.6.back_ref
  117.3 0.0 collective-permute-done.7.direct_ref
  117.3 0.9 shard_map.91
  118.2 11.4 %all-to-all-done.1.received_ref = bf16[16,16,128]{2,1,0:T(8,128)(2,1)S(1)} async-done(((bf16[16,16,128]{2,1,0:T(8,128)(2,1)}), bf16[16,16,128]{2,1,0:T(8,128)(2,1)S(1)}, u32[]{:S(2)}, u32[]{:S(2)}) %all-to-all-start.1) | async-done | bytes 65568 | tf_op jit(solution)/shard_map/all_to_all | solution.py:315
  129.5 0.6 shard_map.94
Async XLA Ops:
  0.6 30.1 %collective-permute-start.4 = (bf16[1024,256]{1,0:T(8,128)(2,1)}, bf16[1024,256]{1,0:T(8,128)(2,1)S(1)}, u32[]{:S(2)}, u32[]{:S(2)}) collective-permute-start(bf16[1024,256]{1,0:T(8,128)(2,1)} %bitcast.4), channel_id=1, source_target_pairs={{0,29},{1,30},{2,31},{3,0},{4,1},{5,2},{6,3},{7,4},{8,5},{9,6},{10... | collective-permute-start | bytes 1572872 | tf_op jit(solution)/shard_map/ppermute | solution.py:27
  11.9 34.6 %collective-permute-start = (bf16[1024,256]{1,0:T(8,128)(2,1)}, bf16[1024,256]{1,0:T(8,128)(2,1)S(1)}, u32[]{:S(2)}, u32[]{:S(2)}) collective-permute-start(bf16[1024,256]{1,0:T(8,128)(2,1)} %bitcast.5), channel_id=1, source_target_pairs={{0,29},{1,30},{2,31},{3,0},{4,1},{5,2},{6,3},{7,4},{8,5},{9,6},{10... | collective-permute-start | bytes 1572872 | tf_op jit(solution)/shard_map/ppermute | solution.py:27
  15.1 35.4 %collective-permute-start.1 = (bf16[1024,256]{1,0:T(8,128)(2,1)}, bf16[1024,256]{1,0:T(8,128)(2,1)S(1)}, u32[]{:S(2)}, u32[]{:S(2)}) collective-permute-start(bf16[1024,256]{1,0:T(8,128)(2,1)} %bitcast.6), channel_id=1, source_target_pairs={{0,5},{1,6},{2,7},{3,8},{4,9},{5,10},{6,11},{7,12},{8,13},{9,14},{... | collective-permute-start | bytes 1572872 | tf_op jit(solution)/shard_map/ppermute | solution.py:27
  30.7 26.4 %collective-permute-start.5 = (bf16[1024,256]{1,0:T(8,128)(2,1)S(1)}, bf16[1024,256]{1,0:T(8,128)(2,1)S(1)}, u32[]{:S(2)}, u32[]{:S(2)}) collective-permute-start(bf16[1024,256]{1,0:T(8,128)(2,1)S(1)} %collective-permute-done.4.cot_ref.refs_9_), channel_id=1, source_target_pairs={{61,29},{62,30},{63,31},{32,0},{33,1},{34,2},{35,3},{36,4},{37,5},... | collective-permute-start | bytes 1572872 | tf_op jit(solution)/shard_map/ppermute | solution.py:27
  32.6 1.0 copy-start
  33.7 1.0 copy-start.1
  34.7 0.9 copy-start.2
  35.6 0.9 copy-start.3
  51.3 15.8 %collective-permute-start.3 = (bf16[1024,256]{1,0:T(8,128)(2,1)S(1)}, bf16[1024,256]{1,0:T(8,128)(2,1)S(1)}, u32[]{:S(2)}, u32[]{:S(2)}) collective-permute-start(bf16[1024,256]{1,0:T(8,128)(2,1)S(1)} %get-tuple-element.21.middle_ref.refs_6_), channel_id=1, source_target_pairs={{61,29},{62,30},{63,31},{32,0},{33,1},{34,2},{35,3},{36,4},{37,5},... | collective-permute-start | bytes 1572872 | tf_op jit(solution)/shard_map/ppermute | solution.py:27
  53.2 15.8 %collective-permute-start.2 = (bf16[1024,256]{1,0:T(8,128)(2,1)S(1)}, bf16[1024,256]{1,0:T(8,128)(2,1)S(1)}, u32[]{:S(2)}, u32[]{:S(2)}) collective-permute-start(bf16[1024,256]{1,0:T(8,128)(2,1)S(1)} %get-tuple-element.21.middle_ref.refs_6_), channel_id=1, source_target_pairs={{29,61},{30,62},{31,63},{0,32},{1,33},{2,34},{3,35},{4,36},{5,37},... | collective-permute-start | bytes 1572872 | tf_op jit(solution)/shard_map/ppermute | solution.py:27
  74.3 31.3 %all-to-all-start = ((bf16[32,2,80,128]{3,2,1,0:T(8,128)(2,1)}), bf16[32,2,80,128]{3,2,1,0:T(8,128)(2,1)S(1)}, u32[]{:S(2)}, u32[]{:S(2)}) async-start(bf16[32,2,80,128]{3,2,1,0:T(8,128)(2,1)} %shard_map.92), calls=%async_computation | async-start | bytes 2621440 | tf_op jit(solution)/shard_map/all_to_all | solution.py:307
  86.7 30.6 %collective-permute-start.6 = (bf16[1024,256]{1,0:T(8,128)(2,1)S(1)}, bf16[1024,256]{1,0:T(8,128)(2,1)S(1)}, u32[]{:S(2)}, u32[]{:S(2)}) collective-permute-start(bf16[1024,256]{1,0:T(8,128)(2,1)S(1)} %get-tuple-element.26), channel_id=1, source_target_pairs={{5,0},{6,1},{7,2},{8,3},{9,4},{10,5},{11,6},{12,7},{13,8},{14,9},{... | collective-permute-start | bytes 1572872 | tf_op jit(solution)/shard_map/ppermute | solution.py:27
  88.6 28.7 %collective-permute-start.7 = (bf16[1024,256]{1,0:T(8,128)(2,1)S(1)}, bf16[1024,256]{1,0:T(8,128)(2,1)S(1)}, u32[]{:S(2)}, u32[]{:S(2)}) collective-permute-start(bf16[1024,256]{1,0:T(8,128)(2,1)S(1)} %get-tuple-element.27), channel_id=1, source_target_pairs={{29,0},{30,1},{31,2},{0,3},{1,4},{2,5},{3,6},{4,7},{5,8},{6,9},{7,... | collective-permute-start | bytes 1572872 | tf_op jit(solution)/shard_map/ppermute | solution.py:27
  106.5 23.1 %all-to-all-start.1 = ((bf16[16,16,128]{2,1,0:T(8,128)(2,1)}), bf16[16,16,128]{2,1,0:T(8,128)(2,1)S(1)}, u32[]{:S(2)}, u32[]{:S(2)}) async-start(bf16[16,16,128]{2,1,0:T(8,128)(2,1)} %shard_map.93), calls=%async_computation.1 | async-start | bytes 131072 | tf_op jit(solution)/shard_map/all_to_all | solution.py:315

commit v6 on v5

--- a/solution.py
+++ b/solution.py
@@ -94,9 +94,15 @@
         ).astype(jnp.bfloat16)
 
 
-def tap_kernel(middle_ref, middle_ahead_ref, gated_ahead_ref, conv_ref, tap_ref):
+def tap_kernel(
+    odd_ref, middle_ref, even_ref, uneven_ref, gated_ahead_ref, conv_ref, tap_ref, past_ref
+):
+    odd = odd_ref[0] == 1
     for part in tiles(middle_ref.shape[0]):
-        t, s = gates(middle_ahead_ref[part], middle_ref[part], conv_ref)
+        first, second = even_ref[part].astype(jnp.float32), uneven_ref[part].astype(jnp.float32)
+        past_ref[part] = jnp.where(odd, first, second).astype(jnp.bfloat16)
+        middle_ahead = jnp.where(odd, second, first).astype(jnp.bfloat16)
+        t, s = gates(middle_ahead, middle_ref[part], conv_ref)
         ahead = gate_gradient(t, s, gated_ahead_ref[part])
         tap_ref[part] = contract_cols(ahead, conv_ref[0]).astype(jnp.bfloat16)
 
@@ -201,10 +207,11 @@
 def call(kernel, outs, *args, scratch=(), flops=0):
     moved = sum(a.size * a.dtype.itemsize for a in (*args, *outs))
     here = pl.BlockSpec(memory_space=pltpu.VMEM)
+    scalar = pl.BlockSpec(memory_space=pltpu.SMEM)
     return pl.pallas_call(
         kernel,
         out_shape=tuple(outs),
-        in_specs=[here] * len(args),
+        in_specs=[scalar if a.dtype == jnp.int32 else here for a in args],
         out_specs=(here,) * len(outs),
         scratch_shapes=list(scratch),
         compiler_params=pltpu.CompilerParams(vmem_limit_bytes=VMEM_LIMIT),
@@ -236,8 +243,9 @@
     single, double = array((rows, channels), f32), array((rows, width), f32)
     x, cot = x.reshape(rows, channels), cotangent.reshape(rows, channels)
     homes = [(i, place(i)) for i in range(blocks)]
+    own_x = move(x, homes)
     past = move(x, [(i, place(j)) for i, j in pairs(near)])
-    x = move(x, homes)
+    x = own_x
     cot = move(cot, homes)
     cot_ahead = move(cot, [(place(i), place(j)) for i, j in pairs(-far)])
     weights = (conv_first, proj_first, conv_second, proj_second)
@@ -258,13 +266,21 @@
         proj_first,
         flops=6 * rows * channels * channels,
     )
-    middle_past = move(middle, [(place(i), place(j)) for i, j in pairs(far)])
-    middle_ahead = move(middle, [(place(i), place(j)) for i, j in pairs(-far)])
-    (tap_second,) = call(
+    swapped = []
+    for odd in range(2):
+        route = [
+            (place(i), place(j)) for i, j in pairs(far) + pairs(-far) if min(i, j) // far % 2 == odd
+        ]
+        swapped.append(move(middle, route))
+    device = lax.axis_index(BLOCKS)
+    block = device // members * members + (device + SHIFT) % members
+    odd = (block // far % 2).astype(jnp.int32).reshape(1)
+    tap_second, middle_past = call(
         tap_kernel,
-        (narrow,),
+        (narrow, narrow),
+        odd,
         middle,
-        middle_ahead,
+        *swapped,
         gated_ahead,
         conv_second,
         flops=12 * rows * channels * channels,

time: 131 us -> 130 us (level)
  starting transfers between devices: 52.4 us -> 47.9 us
  waiting for transfers between devices: 62.5 us -> 65.8 us
    ppermute x8, waiting for transfers between devices: 37.3 us -> 41 us  [move(): return lax.ppermute(block, BLOCKS, route)]
    all_to_all x1, starting transfers between devices: 12.4 us -> 10.2 us  [per_device(): received = lax.all_to_all(sent, ('dp', 'group', 'core'), 0, 0, tiled=True)]
  transfers between devices with their start and end apart: 10 -> 10, of which waited for: 8 -> 8; matrix products, arithmetic and copies ran while one was open for 0% -> 0% of each run, Pallas kernels for 4% -> 3%
where the time goes in v6:
time: 130 us; the launch traced here: 129 us
  waiting for transfers between devices  65.8 us (51%)
  starting transfers between devices  47.9 us (37%)
  Pallas kernels  10.6 us (8%)
  local copies, waits for them, and re-layouts  3.88 us (3%)
    ppermute x8, waiting for transfers between devices, move(): return lax.ppermute(block, BLOCKS, route)  41 us
    ppermute x8, starting transfers between devices, move(): return lax.ppermute(block, BLOCKS, route)  28.9 us
    all_to_all x1, waiting for transfers between devices, per_device(): received = lax.all_to_all(sent, ('dp', 'group', 'core'), 0, 0, tiled=True)  14.5 us
    pallas_call x10, Pallas kernels, call(): pl.pallas_call(kernel, out_shape=tuple(outs), in_specs=[scalar if a.dtype...  10.6 us
    all_to_all x1, waiting for transfers between devices, per_device(): received = lax.all_to_all(sent, 'ring', 0, 0, tiled=True)  10.3 us
    all_to_all x1, starting transfers between devices, per_device(): received = lax.all_to_all(sent, ('dp', 'group', 'core'), 0, 0, tiled=True)  10.2 us
    all_to_all x1, starting transfers between devices, per_device(): received = lax.all_to_all(sent, 'ring', 0, 0, tiled=True)  8.81 us
    unnamed x8, local copies, waits for them, and re-layouts  3.88 us
  transfers between devices with their start and end apart: 10, of which 8 were waited for; matrix products, arithmetic and copies ran while one was open for 0% of the time, Pallas kernels for 3%

profile of v6, /device:TPU:2, one launch (start us, length us, event | category | flops | bytes accessed | tf_op | source)
XLA Modules:
  0.0 129.0 jit_solution(13693254933461436495)
XLA Ops:
  0.6 11.3 %collective-permute-start.4 = (bf16[1024,256]{1,0:T(8,128)(2,1)}, bf16[1024,256]{1,0:T(8,128)(2,1)S(1)}, u32[]{:S(2)}, u32[]{:S(2)}) collective-permute-start(bf16[1024,256]{1,0:T(8,128)(2,1)} %bitcast.5), channel_id=1, source_target_pairs={{0,29},{1,30},{2,31},{3,0},{4,1},{5,2},{6,3},{7,4},{8,5},{9,6},{10... | collective-permute-start | bytes 1572872 | tf_op jit(solution)/shard_map/ppermute | solution.py:27
  11.9 3.2 %collective-permute-start = (bf16[1024,256]{1,0:T(8,128)(2,1)}, bf16[1024,256]{1,0:T(8,128)(2,1)S(1)}, u32[]{:S(2)}, u32[]{:S(2)}) collective-permute-start(bf16[1024,256]{1,0:T(8,128)(2,1)} %bitcast.6), channel_id=1, source_target_pairs={{0,29},{1,30},{2,31},{3,0},{4,1},{5,2},{6,3},{7,4},{8,5},{9,6},{10... | collective-permute-start | bytes 1572872 | tf_op jit(solution)/shard_map/ppermute | solution.py:27
  15.1 2.8 %collective-permute-start.1 = (bf16[1024,256]{1,0:T(8,128)(2,1)}, bf16[1024,256]{1,0:T(8,128)(2,1)S(1)}, u32[]{:S(2)}, u32[]{:S(2)}) collective-permute-start(bf16[1024,256]{1,0:T(8,128)(2,1)} %bitcast.7), channel_id=1, source_target_pairs={{0,5},{1,6},{2,7},{3,8},{4,9},{5,10},{6,11},{7,12},{8,13},{9,14},{... | collective-permute-start | bytes 1572872 | tf_op jit(solution)/shard_map/ppermute | solution.py:27
  18.0 12.8 %collective-permute-done.4.cot_ref.refs_9_ = bf16[1024,256]{1,0:T(8,128)(2,1)S(1)} collective-permute-done((bf16[1024,256]{1,0:T(8,128)(2,1)}, bf16[1024,256]{1,0:T(8,128)(2,1)S(1)}, u32[]{:S(2)}, u32[]{:S(2)}) %collective-permute-start.4) | collective-permute-done | bytes 524320 | tf_op jit(solution)/shard_map/ppermute | solution.py:27
  30.7 1.9 %collective-permute-start.5 = (bf16[1024,256]{1,0:T(8,128)(2,1)S(1)}, bf16[1024,256]{1,0:T(8,128)(2,1)S(1)}, u32[]{:S(2)}, u32[]{:S(2)}) collective-permute-start(bf16[1024,256]{1,0:T(8,128)(2,1)S(1)} %collective-permute-done.4.cot_ref.refs_9_), channel_id=1, source_target_pairs={{61,29},{62,30},{63,31},{32,0},{33,1},{34,2},{35,3},{36,4},{37,5},... | collective-permute-start | bytes 1572872 | tf_op jit(solution)/shard_map/ppermute | solution.py:27
  32.7 0.0 copy-start
  32.7 1.0 copy-done
  33.7 0.0 copy-start.1
  33.7 1.0 copy-done.1
  34.8 0.0 copy-start.2
  34.8 0.9 copy-done.2
  35.7 0.0 copy-start.3
  35.7 0.9 copy-done.3
  36.6 0.1 shard_map.85
  36.7 9.9 %collective-permute-done.x_ref.refs_1_ = bf16[1024,256]{1,0:T(8,128)(2,1)S(1)} collective-permute-done((bf16[1024,256]{1,0:T(8,128)(2,1)}, bf16[1024,256]{1,0:T(8,128)(2,1)S(1)}, u32[]{:S(2)}, u32[]{:S(2)}) %collective-permute-start) | collective-permute-done | bytes 524320 | tf_op jit(solution)/shard_map/ppermute | solution.py:27
  46.5 0.4 shard_map.86.own_ref
  47.0 3.6 %collective-permute-done.1.past_ref.refs_0_ = bf16[1024,256]{1,0:T(8,128)(2,1)S(1)} collective-permute-done((bf16[1024,256]{1,0:T(8,128)(2,1)}, bf16[1024,256]{1,0:T(8,128)(2,1)S(1)}, u32[]{:S(2)}, u32[]{:S(2)}) %collective-permute-start.1) | collective-permute-done | bytes 524320 | tf_op jit(solution)/shard_map/ppermute | solution.py:27
  50.6 0.7 shard_map.87
  51.3 3.4 %collective-permute-start.3 = (bf16[1024,256]{1,0:T(8,128)(2,1)S(1)}, bf16[1024,256]{1,0:T(8,128)(2,1)S(1)}, u32[]{:S(2)}, u32[]{:S(2)}) collective-permute-start(bf16[1024,256]{1,0:T(8,128)(2,1)S(1)} %get-tuple-element.23.middle_ref.refs_6_), channel_id=1, source_target_pairs={{61,93},{62,94},{63,95},{32,64},{33,65},{34,66},{35,67},{36,68},{3... | collective-permute-start | bytes 1572872 | tf_op jit(solution)/shard_map/ppermute | solution.py:27
  54.7 1.9 %collective-permute-start.2 = (bf16[1024,256]{1,0:T(8,128)(2,1)S(1)}, bf16[1024,256]{1,0:T(8,128)(2,1)S(1)}, u32[]{:S(2)}, u32[]{:S(2)}) collective-permute-start(bf16[1024,256]{1,0:T(8,128)(2,1)S(1)} %get-tuple-element.23.middle_ref.refs_6_), channel_id=1, source_target_pairs={{29,61},{30,62},{31,63},{0,32},{1,33},{2,34},{3,35},{4,36},{5,37},... | collective-permute-start | bytes 1572872 | tf_op jit(solution)/shard_map/ppermute | solution.py:27
  56.6 0.0 collective-permute-done.5.cot_ref
  56.6 0.3 shard_map.88.gated_ahead_ref
  56.9 10.1 %collective-permute-done.3.uneven_ref = bf16[1024,256]{1,0:T(8,128)(2,1)S(1)} collective-permute-done((bf16[1024,256]{1,0:T(8,128)(2,1)S(1)}, bf16[1024,256]{1,0:T(8,128)(2,1)S(1)}, u32[]{:S(2)}, u32[]{:S(2)}) %collective-permute-start.3) | collective-permute-done | bytes 524320 | tf_op jit(solution)/shard_map/ppermute | solution.py:27
  67.0 2.9 %collective-permute-done.2.even_ref = bf16[1024,256]{1,0:T(8,128)(2,1)S(1)} collective-permute-done((bf16[1024,256]{1,0:T(8,128)(2,1)S(1)}, bf16[1024,256]{1,0:T(8,128)(2,1)S(1)}, u32[]{:S(2)}, u32[]{:S(2)}) %collective-permute-start.2) | collective-permute-done | bytes 524320 | tf_op jit(solution)/shard_map/ppermute | solution.py:27
  69.9 1.3 %shard_map.89 = (bf16[1024,256]{1,0:T(8,128)(2,1)S(1)}, bf16[1024,256]{1,0:T(8,128)(2,1)S(1)}) custom-call(s32[1]{0:T(128)} %bitcast.1.odd_ref, bf16[1024,256]{1,0:T(8,128)(2,1)S(1)} %get-tuple-element.23.middle_ref.refs_6_, bf16[1024,256]{1,0:T(8,128)(2,1)S(1)} %collective-permute-done.2.even_ref, bf16[1024,256]{1,0:T(8,128)(2,1)S(1)} %collective-permute-done.3.uneven_ref, ...), custom_call_target="tpu_custom_call" | custom-call | flops 805306368 | bytes 4194308 | tf_op jit(solution)/shard_map/pallas_call | solution.py:211
  71.3 2.5 %shard_map.90 = (bf16[1024,256]{1,0:T(8,128)(2,1)S(1)}, bf16[1024,256]{1,0:T(8,128)(2,1)S(1)}, bf16[1024,256]{1,0:T(8,128)(2,1)S(1)}, bf16[1024,512]{1,0:T(8,128...) custom-call(bf16[1024,256]{1,0:T(8,128)(2,1)S(1)} %get-tuple-element.23.middle_ref.refs_6_, ...), custom_call_target="tpu_custom_call" | custom-call | flops 1744830464 | bytes 9699328 | tf_op jit(solution)/shard_map/pallas_call | solution.py:211
  73.8 2.8 %shard_map.92 = bf16[32,2,80,128]{3,2,1,0:T(8,128)(2,1)} custom-call(bf16[1024,256]{1,0:T(8,128)(2,1)S(1)} %collective-permute-done.1.past_ref.refs_0_, bf16[1024,256]{1,0:T(8,128)(2,1)S(1)} %collective-permute-done.x_ref.refs_1_, bf16[1024,512]{1,0:T(8,128)(2,1)S(1)} %get-tuple-element.32.refs_2_, bf16[1024,256]{1,0:T(8,128)(2,1)S(1)} %get-tuple-element.33.refs_3_, ...), custom_call_target="tpu_custom_call" | custom-call | flops 1342177280 | bytes 7602176 | tf_op jit(solution)/shard_map/pallas_call | solution.py:211
  76.6 10.2 %all-to-all-start = ((bf16[32,2,80,128]{3,2,1,0:T(8,128)(2,1)}), bf16[32,2,80,128]{3,2,1,0:T(8,128)(2,1)S(1)}, u32[]{:S(2)}, u32[]{:S(2)}) async-start(bf16[32,2,80,128]{3,2,1,0:T(8,128)(2,1)} %shard_map.92), calls=%async_computation | async-start | bytes 2621440 | tf_op jit(solution)/shard_map/all_to_all | solution.py:323
  86.8 1.9 %collective-permute-start.6 = (bf16[1024,256]{1,0:T(8,128)(2,1)S(1)}, bf16[1024,256]{1,0:T(8,128)(2,1)S(1)}, u32[]{:S(2)}, u32[]{:S(2)}) collective-permute-start(bf16[1024,256]{1,0:T(8,128)(2,1)S(1)} %get-tuple-element.30), channel_id=1, source_target_pairs={{5,0},{6,1},{7,2},{8,3},{9,4},{10,5},{11,6},{12,7},{13,8},{14,9},{... | collective-permute-start | bytes 1572872 | tf_op jit(solution)/shard_map/ppermute | solution.py:27
  88.7 2.4 %collective-permute-start.7 = (bf16[1024,256]{1,0:T(8,128)(2,1)S(1)}, bf16[1024,256]{1,0:T(8,128)(2,1)S(1)}, u32[]{:S(2)}, u32[]{:S(2)}) collective-permute-start(bf16[1024,256]{1,0:T(8,128)(2,1)S(1)} %get-tuple-element.31), channel_id=1, source_target_pairs={{29,0},{30,1},{31,2},{0,3},{1,4},{2,5},{3,6},{4,7},{5,8},{6,9},{7,... | collective-permute-start | bytes 1572872 | tf_op jit(solution)/shard_map/ppermute | solution.py:27
  91.2 14.5 %all-to-all-done.received_ref = bf16[32,2,80,128]{3,2,1,0:T(8,128)(2,1)S(1)} async-done(((bf16[32,2,80,128]{3,2,1,0:T(8,128)(2,1)}), bf16[32,2,80,128]{3,2,1,0:T(8,128)(2,1)S(1)}, u32[]{:S(2)}, u32[]{:S(2)}) %all-to-all-start) | async-done | bytes 1310752 | tf_op jit(solution)/shard_map/all_to_all | solution.py:323
  105.7 0.9 shard_map.93
  106.6 8.8 %all-to-all-start.1 = ((bf16[16,16,128]{2,1,0:T(8,128)(2,1)}), bf16[16,16,128]{2,1,0:T(8,128)(2,1)S(1)}, u32[]{:S(2)}, u32[]{:S(2)}) async-start(bf16[16,16,128]{2,1,0:T(8,128)(2,1)} %shard_map.93), calls=%async_computation.1 | async-start | bytes 131072 | tf_op jit(solution)/shard_map/all_to_all | solution.py:331
  115.4 1.8 %collective-permute-done.6.back_ref = bf16[1024,256]{1,0:T(8,128)(2,1)S(1)} collective-permute-done((bf16[1024,256]{1,0:T(8,128)(2,1)S(1)}, bf16[1024,256]{1,0:T(8,128)(2,1)S(1)}, u32[]{:S(2)}, u32[]{:S(2)}) %collective-permute-start.6) | collective-permute-done | bytes 524320 | tf_op jit(solution)/shard_map/ppermute | solution.py:27
  117.2 0.0 collective-permute-done.7.direct_ref
  117.2 0.9 shard_map.91
  118.2 10.3 %all-to-all-done.1.received_ref = bf16[16,16,128]{2,1,0:T(8,128)(2,1)S(1)} async-done(((bf16[16,16,128]{2,1,0:T(8,128)(2,1)}), bf16[16,16,128]{2,1,0:T(8,128)(2,1)S(1)}, u32[]{:S(2)}, u32[]{:S(2)}) %all-to-all-start.1) | async-done | bytes 65568 | tf_op jit(solution)/shard_map/all_to_all | solution.py:331
  128.4 0.6 shard_map.94
Async XLA Ops:
  0.6 30.1 %collective-permute-start.4 = (bf16[1024,256]{1,0:T(8,128)(2,1)}, bf16[1024,256]{1,0:T(8,128)(2,1)S(1)}, u32[]{:S(2)}, u32[]{:S(2)}) collective-permute-start(bf16[1024,256]{1,0:T(8,128)(2,1)} %bitcast.5), channel_id=1, source_target_pairs={{0,29},{1,30},{2,31},{3,0},{4,1},{5,2},{6,3},{7,4},{8,5},{9,6},{10... | collective-permute-start | bytes 1572872 | tf_op jit(solution)/shard_map/ppermute | solution.py:27
  11.9 34.6 %collective-permute-start = (bf16[1024,256]{1,0:T(8,128)(2,1)}, bf16[1024,256]{1,0:T(8,128)(2,1)S(1)}, u32[]{:S(2)}, u32[]{:S(2)}) collective-permute-start(bf16[1024,256]{1,0:T(8,128)(2,1)} %bitcast.6), channel_id=1, source_target_pairs={{0,29},{1,30},{2,31},{3,0},{4,1},{5,2},{6,3},{7,4},{8,5},{9,6},{10... | collective-permute-start | bytes 1572872 | tf_op jit(solution)/shard_map/ppermute | solution.py:27
  15.1 35.4 %collective-permute-start.1 = (bf16[1024,256]{1,0:T(8,128)(2,1)}, bf16[1024,256]{1,0:T(8,128)(2,1)S(1)}, u32[]{:S(2)}, u32[]{:S(2)}) collective-permute-start(bf16[1024,256]{1,0:T(8,128)(2,1)} %bitcast.7), channel_id=1, source_target_pairs={{0,5},{1,6},{2,7},{3,8},{4,9},{5,10},{6,11},{7,12},{8,13},{9,14},{... | collective-permute-start | bytes 1572872 | tf_op jit(solution)/shard_map/ppermute | solution.py:27
  30.7 25.9 %collective-permute-start.5 = (bf16[1024,256]{1,0:T(8,128)(2,1)S(1)}, bf16[1024,256]{1,0:T(8,128)(2,1)S(1)}, u32[]{:S(2)}, u32[]{:S(2)}) collective-permute-start(bf16[1024,256]{1,0:T(8,128)(2,1)S(1)} %collective-permute-done.4.cot_ref.refs_9_), channel_id=1, source_target_pairs={{61,29},{62,30},{63,31},{32,0},{33,1},{34,2},{35,3},{36,4},{37,5},... | collective-permute-start | bytes 1572872 | tf_op jit(solution)/shard_map/ppermute | solution.py:27
  32.7 1.0 copy-start
  33.7 1.0 copy-start.1
  34.8 0.9 copy-start.2
  35.7 0.9 copy-start.3
  51.3 15.8 %collective-permute-start.3 = (bf16[1024,256]{1,0:T(8,128)(2,1)S(1)}, bf16[1024,256]{1,0:T(8,128)(2,1)S(1)}, u32[]{:S(2)}, u32[]{:S(2)}) collective-permute-start(bf16[1024,256]{1,0:T(8,128)(2,1)S(1)} %get-tuple-element.23.middle_ref.refs_6_), channel_id=1, source_target_pairs={{61,93},{62,94},{63,95},{32,64},{33,65},{34,66},{35,67},{36,68},{3... | collective-permute-start | bytes 1572872 | tf_op jit(solution)/shard_map/ppermute | solution.py:27
  54.7 15.2 %collective-permute-start.2 = (bf16[1024,256]{1,0:T(8,128)(2,1)S(1)}, bf16[1024,256]{1,0:T(8,128)(2,1)S(1)}, u32[]{:S(2)}, u32[]{:S(2)}) collective-permute-start(bf16[1024,256]{1,0:T(8,128)(2,1)S(1)} %get-tuple-element.23.middle_ref.refs_6_), channel_id=1, source_target_pairs={{29,61},{30,62},{31,63},{0,32},{1,33},{2,34},{3,35},{4,36},{5,37},... | collective-permute-start | bytes 1572872 | tf_op jit(solution)/shard_map/ppermute | solution.py:27
  76.6 29.1 %all-to-all-start = ((bf16[32,2,80,128]{3,2,1,0:T(8,128)(2,1)}), bf16[32,2,80,128]{3,2,1,0:T(8,128)(2,1)S(1)}, u32[]{:S(2)}, u32[]{:S(2)}) async-start(bf16[32,2,80,128]{3,2,1,0:T(8,128)(2,1)} %shard_map.92), calls=%async_computation | async-start | bytes 2621440 | tf_op jit(solution)/shard_map/all_to_all | solution.py:323
  86.8 30.4 %collective-permute-start.6 = (bf16[1024,256]{1,0:T(8,128)(2,1)S(1)}, bf16[1024,256]{1,0:T(8,128)(2,1)S(1)}, u32[]{:S(2)}, u32[]{:S(2)}) collective-permute-start(bf16[1024,256]{1,0:T(8,128)(2,1)S(1)} %get-tuple-element.30), channel_id=1, source_target_pairs={{5,0},{6,1},{7,2},{8,3},{9,4},{10,5},{11,6},{12,7},{13,8},{14,9},{... | collective-permute-start | bytes 1572872 | tf_op jit(solution)/shard_map/ppermute | solution.py:27
  88.7 28.5 %collective-permute-start.7 = (bf16[1024,256]{1,0:T(8,128)(2,1)S(1)}, bf16[1024,256]{1,0:T(8,128)(2,1)S(1)}, u32[]{:S(2)}, u32[]{:S(2)}) collective-permute-start(bf16[1024,256]{1,0:T(8,128)(2,1)S(1)} %get-tuple-element.31), channel_id=1, source_target_pairs={{29,0},{30,1},{31,2},{0,3},{1,4},{2,5},{3,6},{4,7},{5,8},{6,9},{7,... | collective-permute-start | bytes 1572872 | tf_op jit(solution)/shard_map/ppermute | solution.py:27
  106.6 21.8 %all-to-all-start.1 = ((bf16[16,16,128]{2,1,0:T(8,128)(2,1)}), bf16[16,16,128]{2,1,0:T(8,128)(2,1)S(1)}, u32[]{:S(2)}, u32[]{:S(2)}) async-start(bf16[16,16,128]{2,1,0:T(8,128)(2,1)} %shard_map.93), calls=%async_computation.1 | async-start | bytes 131072 | tf_op jit(solution)/shard_map/all_to_all | solution.py:331
